TPU v7x, 512 devices: a whole 4x4x16 slice. The times are simulated.
512 devices in a mesh: dp: 64 (over z, y_hi, core), replica: 8 (over y_lo, x).
Axes of the slice: x: 4, y: 4 (y_hi: 2, y_lo: 2; y = y_hi * 2 + y_lo), z: 16, core: 2. Of those that a mesh axis runs over, the one named last changes fastest.
Arguments:
- img_emb: bfloat16 [8, 8192, 768], P('replica', 'dp')
- txt_base: bfloat16 [8, 8192, 768], P('replica', 'dp')
- txt_feat: bfloat16 [8, 8192, 640], P('replica', 'dp'), may hold values from -6 to 6
- head: float32 [640, 768], P('dp'), may hold values from -0.25 to 0.25
- momentum: float32 [640, 768], P('dp'), may hold values from -3 to 3
- positive_image: int32 [8, 8192], P('replica', 'dp'), may hold values from 0 to 8191, each once within a row
Outputs:
- new_head: float32 [640, 768], P('dp')
- new_momentum: float32 [640, 768], P('dp')
Inputs may be any that keep to these rules, and one draw needn't show every extreme that they name: `positive_image`: in each replica the 8192 texts name 8192 different images.
All inputs are finite; a program needn't handle non-finite values.
Results may differ from a plain program's by a relative error of at most 0.005.
Values may be sent and summed in bfloat16 or wider, within the bound.
A program may use at most 64 MiB of HBM per device.

v0:
```python
import jax
import jax.numpy as jnp
from jax import lax
from jax.sharding import PartitionSpec as P

logit_scale = 10.0
logit_bias = -3.0
norm_epsilon = 1e-06
momentum_decay = 0.9
blend_weight = 0.7
outer_rate = 0.7


def per_device(img_emb, txt_base, txt_feat, head, momentum, positive_image):
    features = txt_feat[0]
    labels = positive_image[0]
    image_wide = img_emb[0].astype(jnp.float32)
    image_unit = (
        image_wide
        * lax.rsqrt(jnp.sum(image_wide * image_wide, axis=1, keepdims=True) + norm_epsilon)
    ).astype(jnp.bfloat16)
    head_low = head.astype(jnp.bfloat16)
    columns = features
    projected = jnp.dot(
        columns,
        lax.all_gather(head_low, "dp", axis=0, tiled=True),
        preferred_element_type=jnp.float32,
    )
    text_emb = txt_base[0].astype(jnp.float32) + projected
    inv_norm = lax.rsqrt(jnp.sum(text_emb * text_emb, axis=1, keepdims=True) + norm_epsilon)
    text_exact = text_emb * inv_norm
    text_unit = text_exact.astype(jnp.bfloat16)
    piece = lax.all_gather(image_unit, "dp", axis=0, tiled=True)
    logits = (
        logit_scale
        * lax.dot_general(
            text_unit, piece, (((1,), (1,)), ((), ())), preferred_element_type=jnp.float32
        )
        + logit_bias
    )
    columns = lax.iota(jnp.int32, piece.shape[0])
    matches = (labels[:, None] == columns[None, :]).astype(jnp.float32)
    weights = (jax.nn.sigmoid(logits) - matches).astype(jnp.bfloat16)
    unit_grad = logit_scale * jnp.dot(weights, piece, preferred_element_type=jnp.float32)
    along = jnp.sum(text_exact * unit_grad, axis=1, keepdims=True)
    text_grad = ((unit_grad - text_exact * along) * inv_norm).astype(jnp.bfloat16)
    share_rows = head.shape[0]
    local_term = lax.dot_general(
        features, text_grad, (((0,), (0,)), ((), ())), preferred_element_type=jnp.float32
    )
    summed = lax.psum(local_term, ("dp", "replica"))
    share = lax.dynamic_slice_in_dim(summed, lax.axis_index("dp") * share_rows, share_rows, 0)
    head_grad = share / lax.axis_size("replica")
    new_momentum = momentum_decay * momentum + (1.0 - momentum_decay) * head_grad
    new_head = head - outer_rate * ((1.0 - blend_weight) * head_grad + blend_weight * new_momentum)
    return (new_head, new_momentum)


def solution(mesh):
    placed = (
        P("replica", "dp", None),
        P("replica", "dp", None),
        P("replica", "dp", None),
        P("dp", None),
        P("dp", None),
        P("replica", "dp"),
    )
    return jax.shard_map(
        per_device,
        mesh=mesh,
        in_specs=placed,
        out_specs=(P("dp", None), P("dp", None)),
        check_vma=False,
    )
```

profile of v0, /device:TPU:6, one launch (start us, length us, event | category | flops | bytes accessed | tf_op | source)
XLA Modules:
  0.0 692.7 jit_solution(11557324892986183658)
XLA Ops:
  7.2 0.0 copy-start
  7.2 0.0 copy-start.1
  7.2 0.0 copy-start.4
  7.2 0.0 all-gather.3.cloned.1.call-start
  7.2 1.2 fusion.9
  8.4 1.7 fusion.10
  10.1 0.0 all-gather.3.cloned.1.call-update
  10.1 0.0 all-reduce.2.cloned.1.call-start
  10.2 0.8 convert_bitcast_fusion
  11.0 89.4 %all-gather = bf16[64,10,768]{2,1,0:T(8,128)(2,1)S(1)} all-gather(bf16[1,10,768]{2,1,0:T(8,128)(2,1)S(1)} %convert_bitcast_fusion), channel_id=1, replica_groups=mesh['dp'=64,'replica'=8] {'dp'}, dimensions={0}, use_global_device_ids=true | all-gather | bytes 998400 | tf_op jit(solution)/shard_map/all_gather | solution.py:26
  100.4 0.4 reshape.25
  100.7 0.0 copy-done
  100.7 0.0 copy-done.1
  100.8 0.4 multiply_reduce_fusion.1
  101.2 94.8 %all-gather.3.cloned.1.call-done = bf16[8192,768]{1,0:T(8,128)(2,1)} async-done(((bf16[128,768]{1,0:T(8,128)(2,1)}), bf16[8192,768]{1,0:T(8,128)(2,1)}) %all-gather.3.cloned.1.call-update) | async-done | bytes 12582928 | tf_op jit(solution)/shard_map/all_gather | solution.py:33
  196.0 0.0 copy-done.4
  196.0 14.1 %multiply_reduce_fusion = (f32[128]{0:T(128)S(1)}, f32[128,768]{1,0:T(8,128)S(1)}) fusion(f32[128,768]{1,0:T(8,128)S(1)} %get-tuple-element.11, f32[128]{0:T(128)S(1)} %add_rsqrt_fusion.1, bf16[8192,768]{1,0:T(8,128)(2,1)} %all-gather.3.cloned.1.call-done, s32[128]{0:T(128)S(1)} %bitcast.22), kind=kOutput, calls=%fused_computation.18 | convolution fusion | flops 3231252480 | bytes 13370880 | tf_op jit(solution)/shard_map/dot_general | solution.py:44
  210.2 0.0 copy-start.2
  210.2 0.0 copy-start.3
  210.2 1.8 convolution_bitcast_fusion
  212.0 0.0 all-reduce.2.cloned.1.call-update
  212.0 472.4 %all-reduce.2.cloned.1.call-done = f32[640,768]{1,0:T(8,128)} async-done(((f32[640,768]{1,0:T(8,128)}), f32[640,768]{1,0:T(8,128)}) %all-reduce.2.cloned.1.call-update) | async-done | bytes 1966096 | tf_op jit(solution)/shard_map/psum | solution.py:51
  684.4 0.0 copy-done.2
  684.4 0.0 copy-done.3
  684.4 1.5 multiply_subtract_fusion
  (2 shorter events, 0.0 us)
Async XLA Ops:
  7.2 93.6 %copy-start = (bf16[1,128,640]{2,1,0:T(8,128)(2,1)S(1)}, bf16[1,128,640]{2,1,0:T(8,128)(2,1)}, u32[]{:S(2)}) copy-start(bf16[1,128,640]{2,1,0:T(8,128)(2,1)} %param.8) | copy-start | bytes 491524
  7.2 93.6 %copy-start.1 = (bf16[1,128,768]{2,1,0:T(8,128)(2,1)S(1)}, bf16[1,128,768]{2,1,0:T(8,128)(2,1)}, u32[]{:S(2)}) copy-start(bf16[1,128,768]{2,1,0:T(8,128)(2,1)} %param.7) | copy-start | bytes 589828
  7.2 188.8 %copy-start.4 = (s32[1,128]{1,0:T(1,128)S(1)}, s32[1,128]{1,0:T(1,128)}, u32[]{:S(2)}) copy-start(s32[1,128]{1,0:T(1,128)} %param.11) | copy-start | bytes 1540
  7.2 188.8 %all-gather.3.cloned.1.call-start = ((), (), s32[]{:S(2)}) async-start(), calls=%async_computation | async-start | bytes 12779520 | tf_op jit(solution)/shard_map/all_gather | solution.py:33
  10.1 674.2 %all-reduce.2.cloned.1.call-start = ((), (), s32[]{:S(2)}) async-start(), calls=%async_computation.1 | async-start | bytes 3932160 | tf_op jit(solution)/shard_map/psum | solution.py:51
  210.2 474.2 %copy-start.2 = (f32[10,768]{1,0:T(8,128)S(1)}, f32[10,768]{1,0:T(8,128)}, u32[]{:S(2)}) copy-start(f32[10,768]{1,0:T(8,128)} %param.9) | copy-start | bytes 92164
  210.2 474.2 %copy-start.3 = (f32[10,768]{1,0:T(8,128)S(1)}, f32[10,768]{1,0:T(8,128)}, u32[]{:S(2)}) copy-start(f32[10,768]{1,0:T(8,128)} %param.10) | copy-start | bytes 92164
Sparse Core Ops, SparseCore 0:
  11.3 184.6 all-gather.2
  212.1 472.1 all-reduce.1
where the time goes:
time: 693 us
  waiting for transfers between devices  567 us (82%)
  blocking collectives  89.4 us (13%)
  matrix products  16.3 us (2%)
  between operations  14.1 us (2%)
    psum x1, waiting for transfers between devices, per_device(): summed = lax.psum(local_term, ('dp', 'replica'))  472 us
    all_gather x1, waiting for transfers between devices, per_device(): piece = lax.all_gather(image_unit, 'dp', axis=0, tiled=True)  94.8 us
    all_gather x1, blocking collectives, per_device(): lax.all_gather(head_low, 'dp', axis=0, tiled=True)  89.4 us
    dot_general x1, matrix products, per_device(): jnp.dot(weights, piece, preferred_element_type=jnp.float32)  14.1 us
  transfers between devices with their start and end apart: 2, of which 2 were waited for; matrix products, arithmetic and copies ran while one was open for 0% of the time, Pallas kernels for 0%

commit v1 on v0

v1 whole, which is shorter than its diff:
```python
import functools

import jax
import jax.numpy as jnp
from jax import lax
from jax.experimental import pallas as pl
from jax.experimental.pallas import tpu as pltpu
from jax.sharding import PartitionSpec as P

MESH = pl.DeviceIdType.MESH
F32 = jnp.float32
BF16 = jnp.bfloat16

logit_scale = 10.0
logit_bias = -3.0
norm_epsilon = 1e-06
momentum_decay = 0.9
blend_weight = 0.7
outer_rate = 0.7

NZ = 16
ROWS = 128
D = 768
K = 640
OWN = 10
PAD = 16
HALF = D // 2
NT = (((1,), (1,)), ((), ()))
CHUNKS = 4
PIECE = ROWS // CHUNKS


def kernel(
    img_hbm,
    base_hbm,
    feat_hbm,
    head_ref,
    momentum_ref,
    label_hbm,
    new_head_ref,
    new_momentum_ref,
    img_raw,
    img,
    tb,
    tf,
    tl,
    hb,
    pick,
    order,
    spread,
    feat_t,
    text_exact,
    text_unit,
    inv_norm,
    label_wide,
    unit_grad,
    grad_low,
    core_out,
    core_in,
    x_own,
    x_out,
    x_in,
    y_out,
    y_in,
    z_out,
    z_in,
    share,
    local_sem,
    up_send,
    up_recv,
    dn_send,
    dn_recv,
    text_send,
    text_recv,
    hz_send,
    hz_recv,
    hy_send,
    hy_recv,
    hx_send,
    hx_recv,
    hc_send,
    hc_recv,
    gc_send,
    gc_recv,
    gx_send,
    gx_recv,
    gy_send,
    gy_recv,
    gz_send,
    gz_recv,
    gb_send,
    gb_recv,
):
    dp = lax.axis_index("dp")
    rep = lax.axis_index("replica")
    z, yh, c = dp // 4, (dp // 2) % 2, dp % 2
    yl, x = rep // 4, rep % 4
    y = yl + 2 * yh

    def at(z2, y2, x2, c2):
        return (z2 * 4 + (y2 // 2) * 2 + c2, (y2 % 2) * 4 + x2)

    def to_z(k):
        return at((z + k) % NZ, y, x, c)

    def to_y(k):
        return at(z, (y + k) % 4, x, c)

    def to_x(k):
        return at(z, y, (x + k) % 4, c)

    to_core = at(z, y, x, 1 - c)

    def remote(src, dst, send, recv, device):
        return pltpu.make_async_remote_copy(
            src_ref=src, dst_ref=dst, send_sem=send, recv_sem=recv, device_id=device, device_id_type=MESH
        )

    loads = [
        pltpu.make_async_copy(img_hbm, img_raw, local_sem.at[0]),
        pltpu.make_async_copy(base_hbm, tb.at[0], local_sem.at[1]),
        pltpu.make_async_copy(feat_hbm, tf.at[0], local_sem.at[2]),
        pltpu.make_async_copy(label_hbm, tl.at[0], local_sem.at[3]),
    ]
    for load in loads:
        load.start()

    barrier = pltpu.get_barrier_semaphore()

    def greet(device):
        pl.semaphore_signal(barrier, inc=1, device_id=device, device_id_type=MESH)

    def greet_z(k, carry):
        greet(to_z(k))
        return carry

    lax.fori_loop(1, NZ, greet_z, 0)
    greet(to_core)
    for k in range(1, 4):
        greet(to_x(k))
        greet(to_y(k))
        greet(at(z, yh * 2 + (1 - yl), (x + k) % 4, c))

    loads[0].wait()
    wide = img_raw[...].astype(F32)
    img[0] = (wide * lax.rsqrt(jnp.sum(wide * wide, axis=1, keepdims=True) + norm_epsilon)).astype(BF16)

    def head_block(c2, x2, yl2, yh2, zh2):
        return (((c2 * 4 + x2) * 2 + yl2) * 2 + yh2) * 2 + zh2

    is_source = (z % 8) == rep
    own_block = head_block(c, x, yl, yh, z // 8)
    head_low = jnp.concatenate([head_ref[...], jnp.zeros((PAD - OWN, D), F32)], axis=0).astype(BF16)

    @pl.when(is_source)
    def _():
        hb[own_block] = head_low

    pl.semaphore_wait(barrier, 15 + 1 + 9)

    def head_z(k):
        block = hb.at[own_block]
        return remote(block, block, hz_send.at[k], hz_recv.at[z // 8], to_z(k))

    @pl.when(is_source)
    def _():
        def go(k, carry):
            head_z(k).start()
            return carry

        lax.fori_loop(1, NZ, go, 0)

    def text_copies(src, slot, device, first):
        return [
            remote(s, d, text_send.at[first + i], text_recv.at[first + i], device)
            for i, (s, d) in enumerate(zip(src, (tb.at[slot], tf.at[slot], tl.at[slot])))
        ]

    own_text = (base_hbm, feat_hbm, label_hbm)
    text_y = text_copies(own_text, 2, to_y(2), 0)
    text_c = text_copies(own_text, 1, to_core, 3)
    text_yc = text_copies((tb.at[2], tf.at[2], tl.at[2]), 3, to_core, 6)
    for copy in text_y:
        copy.start()

    def up(s, k):
        rows = pl.ds(k * PIECE, PIECE)
        src, dst = jnp.maximum(2 * s - 3, 0), 2 * s - 1
        return remote(img.at[src, rows], img.at[dst, rows], up_send.at[s, k], up_recv.at[s, k], to_z(1))

    def dn(s, k):
        rows = pl.ds(k * PIECE, PIECE)
        src, dst = 2 * s - 2, jnp.minimum(2 * s, 15)
        return remote(img.at[src, rows], img.at[dst, rows], dn_send.at[s, k], dn_recv.at[s, k], to_z(NZ - 1))

    for k in range(CHUNKS):
        up(1, k).start()
        dn(1, k).start()
    for copy in text_c:
        copy.start()

    def ring(s):
        for k in range(CHUNKS):
            up(s, k).wait_recv()

            @pl.when((s < 7) | (k < CHUNKS // 2))
            def _():
                up(s + 1, k).start()

            dn(s, k).wait_recv()

            @pl.when((s < 7) | (k >= CHUNKS // 2))
            def _():
                dn(s + 1, k).start()

    place = lax.broadcasted_iota(jnp.int32, (1, 64 * PAD), 1)
    block, row = place >> 4, place & 15
    source = ((block >> 3) & 3) + 4 * ((block >> 2) & 1) + 8 * (block & 1)
    wanted = (source * 4 + ((block >> 1) & 1) * 2 + (block >> 5)) * OWN + row
    wanted = jnp.where(row < OWN, wanted, -1)
    pick[...] = (lax.broadcasted_iota(jnp.int32, (K, 64 * PAD), 0) == wanted).astype(F32).astype(BF16)

    place = lax.broadcasted_iota(jnp.int32, (K, 1), 0)
    block = (place * 6554) >> 16
    row = place - block * OWN
    source = ((block >> 4) & 1) * 2 + ((block >> 2) & 1) + 4 * (block & 3)
    owner = source * 4 + ((block >> 3) & 1) * 2 + (c ^ 1 ^ (block >> 5))
    wanted = owner * OWN + row
    order[...] = (lax.broadcasted_iota(jnp.int32, (K, K), 1) == wanted).astype(F32).astype(BF16)

    for zh in range(2):

        @pl.when(z != rep + 8 * zh)
        def _():
            block = hb.at[head_block(c, x, yl, yh, zh)]
            remote(block, block, hz_send.at[0], hz_recv.at[zh], to_z(1)).wait_recv()

    def head_y(k):
        blocks = hb.at[pl.ds(head_block(c, x, yl, yh, 0), 2)]
        return remote(blocks, blocks, hy_send.at[k], hy_recv.at[k], to_y(k))

    def head_x(k):
        blocks = hb.at[pl.ds(head_block(c, x, 0, 0, 0), 8)]
        return remote(blocks, blocks, hx_send.at[k], hx_recv.at[k], to_x(k))

    all_mine = hb.at[pl.ds(c * 32, 32)]
    head_c = remote(all_mine, all_mine, hc_send, hc_recv, to_core)

    for k in range(1, 4):
        head_y(k).start()
    ring(1)
    for k in range(1, 4):
        head_y(k).wait_recv()
    for k in range(1, 4):
        head_x(k).start()
    ring(2)
    for copy in text_y:
        copy.wait_recv()
    for copy in text_yc:
        copy.start()
    for k in range(1, 4):
        head_x(k).wait_recv()
    head_c.start()
    ring(3)

    for load in loads[1:]:
        load.wait()
    for copy in text_c + text_yc:
        copy.wait_recv()
    features = tf[...].reshape(4 * ROWS, K)
    spread[...] = jnp.dot(features, pick[...], preferred_element_type=F32).astype(BF16)
    feat_t[...] = lax.dot_general(order[...], features, NT, preferred_element_type=F32).astype(BF16)
    diagonal = lax.broadcasted_iota(jnp.int32, (ROWS, ROWS), 0) == lax.broadcasted_iota(jnp.int32, (ROWS, ROWS), 1)
    for i in range(4):
        column = jnp.sum(jnp.where(diagonal, tl[i].astype(F32), 0.0), axis=1, keepdims=True)
        label_wide[pl.ds(i * ROWS, ROWS)] = jnp.broadcast_to(column, (ROWS, ROWS)).astype(jnp.int32)
    head_c.wait_recv()
    head_all = hb[...].reshape(64 * PAD, D)
    for i in range(4):
        rows = pl.ds(i * ROWS, ROWS)
        emb = tb[i].astype(F32) + jnp.dot(spread[rows], head_all, preferred_element_type=F32)
        inv = lax.rsqrt(jnp.sum(emb * emb, axis=1, keepdims=True) + norm_epsilon)
        exact = emb * inv
        inv_norm[rows] = inv
        text_exact[rows] = exact
        text_unit[rows] = exact.astype(BF16)

    lane = lax.broadcasted_iota(jnp.int32, (1, ROWS), 1)

    def columns(z2):
        return ((z2 % NZ) * 4 + yh * 2 + c) * ROWS + lane

    def process(images, marks, fresh):
        for i in range(2):
            rows = pl.ds(i * 256, 256)
            raw = lax.dot_general(text_unit[rows], images, NT, preferred_element_type=F32)
            chance = 0.5 * jnp.tanh((0.5 * logit_scale) * raw + 0.5 * logit_bias) + 0.5
            labels = label_wide[rows]
            match = jnp.concatenate([(labels == m) for m in marks], axis=1)
            weights = jnp.where(match, chance - 1.0, chance).astype(BF16)
            grad = jnp.dot(weights, images, preferred_element_type=F32)
            if fresh:
                unit_grad[rows] = grad
            else:
                unit_grad[rows] += grad

    process(img[0], [columns(z)], True)

    def pair(p, carry):
        @pl.when(p % 2 == 1)
        def _():
            ring(4 + p // 2)

        images = img[pl.ds(2 * p - 1, 2)].reshape(2 * ROWS, D)
        process(images, [columns(z - p + NZ), columns(z + p)], False)
        return carry

    lax.fori_loop(1, 8, pair, 0)
    for k in range(CHUNKS // 2):
        up(8, k).wait_recv()
        dn(8, k + CHUNKS // 2).wait_recv()
    process(img[15], [columns(z + 8)], False)

    for i in range(4):
        rows = pl.ds(i * ROWS, ROWS)
        exact, grad = text_exact[rows], unit_grad[rows]
        along = jnp.sum(exact * grad, axis=1, keepdims=True)
        grad_low[rows] = ((grad - exact * along) * (logit_scale * inv_norm[rows])).astype(BF16)

    def to_other(h):
        return remote(core_out.at[h], core_in.at[h], gc_send.at[h], gc_recv.at[h], to_core)

    for h in range(2):
        core_out[h] = jnp.dot(feat_t[pl.ds(h * 160, 160)], grad_low[...], preferred_element_type=F32).astype(BF16)
        to_other(h).start()
    for h in range(2):
        mine = jnp.dot(feat_t[pl.ds(320 + h * 160, 160)], grad_low[...], preferred_element_type=F32)
        to_other(h).wait_recv()
        mine += core_in[h].astype(F32)
        for side in range(2):
            part = mine[:, side * HALF : (side + 1) * HALF]
            x_own[2 * h + side] = part
            x_out[2 * h + side] = part.astype(BF16)

    def to_x_part(k):
        return remote(x_out.at[(x + k) % 4], x_in.at[k - 1], gx_send.at[k], gx_recv.at[k], to_x(k))

    for k in range(1, 4):
        to_x_part(k).start()
    total = x_own[x]
    for k in range(1, 4):
        to_x_part(k).wait_recv()
        total += x_in[k - 1].astype(F32)
    for k in range(4):
        y_out[k] = total[k * 40 : (k + 1) * 40]

    def to_y_part(k):
        return remote(y_out.at[(y + k) % 4], y_in.at[k - 1], gy_send.at[k], gy_recv.at[k], to_y(k))

    for k in range(1, 4):
        to_y_part(k).start()
    total = y_out[y]
    for k in range(1, 4):
        to_y_part(k).wait_recv()
        total += y_in[k - 1]
    for j in range(4):
        z_out[j] = jnp.concatenate([total[j * OWN : (j + 1) * OWN], jnp.zeros((PAD - OWN, HALF), F32)], axis=0)

    group = 2 * (x // 2) + yl

    def to_z_part(j):
        k = (group + 4 * j - z + NZ) % NZ
        return remote(z_out.at[j], z_in.at[k], gz_send.at[j], gz_recv.at[k], to_z(k))

    for j in range(4):

        @pl.when(z != group + 4 * j)
        def _():
            to_z_part(j).start()

    is_owner = (z % 4) == group
    side = x % 2

    def to_share(i):
        rep2 = (rep + i) % 8
        device = (dp, rep2)
        return remote(share.at[side], share.at[side], gb_send.at[i], gb_recv.at[side], device)

    @pl.when(is_owner)
    def _():
        z_in[0] = z_out[z // 4]
        for k in range(1, NZ):
            remote(z_out.at[0], z_in.at[k], gz_send.at[0], gz_recv.at[k], to_z(1)).wait_recv()
        share[side] = jnp.sum(z_in[...], axis=0)
        for i in range(1, 8):
            to_share(i).start()

    for s in range(2):

        @pl.when(jnp.logical_not(is_owner & (side == s)))
        def _():
            remote(share.at[s], share.at[s], gb_send.at[0], gb_recv.at[s], to_x(1)).wait_recv()

    head_grad = jnp.concatenate([share[0, :OWN], share[1, :OWN]], axis=1) * (1.0 / 8.0)
    momentum = momentum_decay * momentum_ref[...] + (1.0 - momentum_decay) * head_grad
    new_momentum_ref[...] = momentum
    new_head_ref[...] = head_ref[...] - outer_rate * ((1.0 - blend_weight) * head_grad + blend_weight * momentum)

    @pl.when(is_source)
    def _():
        def drain(k, carry):
            head_z(k).wait_send()
            return carry

        lax.fori_loop(1, NZ, drain, 0)

    for copy in text_y + text_c + text_yc + [head_c]:
        copy.wait_send()

    def drain_ring(s, carry):
        for k in range(CHUNKS):
            up(s, k).wait_send()
            dn(s, k).wait_send()
        return carry

    lax.fori_loop(1, 8, drain_ring, 0)
    for k in range(CHUNKS // 2):
        up(8, k).wait_send()
        dn(8, k + CHUNKS // 2).wait_send()
    for k in range(1, 4):
        head_y(k).wait_send()
        head_x(k).wait_send()
        to_x_part(k).wait_send()
        to_y_part(k).wait_send()
    for h in range(2):
        to_other(h).wait_send()
    for j in range(4):

        @pl.when(z != group + 4 * j)
        def _():
            to_z_part(j).wait_send()

    @pl.when(is_owner)
    def _():
        for i in range(1, 8):
            to_share(i).wait_send()


def per_device(img_emb, txt_base, txt_feat, head, momentum, positive_image):
    vmem = pl.BlockSpec(memory_space=pltpu.VMEM)
    hbm = pl.BlockSpec(memory_space=pl.ANY)
    dma = pltpu.SemaphoreType.DMA
    texts = 4 * ROWS
    out = jax.ShapeDtypeStruct((OWN, D), F32)
    return pl.pallas_call(
        kernel,
        out_shape=(out, out),
        in_specs=[hbm, hbm, hbm, vmem, vmem, hbm],
        out_specs=(vmem, vmem),
        scratch_shapes=[
            pltpu.VMEM((ROWS, D), BF16),
            pltpu.VMEM((NZ, ROWS, D), BF16),
            pltpu.VMEM((4, ROWS, D), BF16),
            pltpu.VMEM((4, ROWS, K), BF16),
            pltpu.VMEM((4, 1, ROWS), jnp.int32),
            pltpu.VMEM((64, PAD, D), BF16),
            pltpu.VMEM((K, 64 * PAD), BF16),
            pltpu.VMEM((K, K), BF16),
            pltpu.VMEM((texts, 64 * PAD), BF16),
            pltpu.VMEM((K, texts), BF16),
            pltpu.VMEM((texts, D), F32),
            pltpu.VMEM((texts, D), BF16),
            pltpu.VMEM((texts, 1), F32),
            pltpu.VMEM((texts, ROWS), jnp.int32),
            pltpu.VMEM((texts, D), F32),
            pltpu.VMEM((texts, D), BF16),
            pltpu.VMEM((2, 160, D), BF16),
            pltpu.VMEM((2, 160, D), BF16),
            pltpu.VMEM((4, 160, HALF), F32),
            pltpu.VMEM((4, 160, HALF), BF16),
            pltpu.VMEM((3, 160, HALF), BF16),
            pltpu.VMEM((4, 40, HALF), F32),
            pltpu.VMEM((3, 40, HALF), F32),
            pltpu.VMEM((4, PAD, HALF), F32),
            pltpu.VMEM((NZ, PAD, HALF), F32),
            pltpu.VMEM((2, PAD, HALF), F32),
            dma((4,)),
            dma((9, CHUNKS)),
            dma((9, CHUNKS)),
            dma((9, CHUNKS)),
            dma((9, CHUNKS)),
            dma((9,)),
            dma((9,)),
            dma((NZ,)),
            dma((2,)),
            dma((4,)),
            dma((4,)),
            dma((4,)),
            dma((4,)),
            dma,
            dma,
            dma((2,)),
            dma((2,)),
            dma((4,)),
            dma((4,)),
            dma((4,)),
            dma((4,)),
            dma((4,)),
            dma((NZ,)),
            dma((8,)),
            dma((2,)),
        ],
        compiler_params=pltpu.CompilerParams(
            collective_id=0, has_side_effects=True, vmem_limit_bytes=48 * 1024 * 1024
        ),
        cost_estimate=pl.CostEstimate(flops=8_000_000_000, bytes_accessed=2_000_000, transcendentals=1_100_000),
        name="contrastive_step",
    )(img_emb[0], txt_base[0], txt_feat[0], head, momentum, positive_image)


def solution(mesh):
    placed = (
        P("replica", "dp", None),
        P("replica", "dp", None),
        P("replica", "dp", None),
        P("dp", None),
        P("dp", None),
        P("replica", "dp"),
    )
    return jax.shard_map(
        per_device,
        mesh=mesh,
        in_specs=placed,
        out_specs=(P("dp", None), P("dp", None)),
        check_vma=False,
    )
```

time: 693 us -> 101 us (0.15)
  waiting for transfers between devices: 567 us -> 0 us
  Pallas kernels: 0 us -> 93.2 us
  blocking collectives: 89.4 us -> 0 us
  matrix products: 16.3 us -> 0 us
  between operations: 14.1 us -> 0.65 us
    psum x1 -> x0, waiting for transfers between devices: 472 us -> none  [per_device(): summed = lax.psum(local_term, ('dp', 'replica'))]
    all_gather x1 -> x0, waiting for transfers between devices: 94.8 us -> none  [per_device(): piece = lax.all_gather(image_unit, 'dp', axis=0, tiled=True)]
    pallas_call x0 -> x1, Pallas kernels: none -> 93.2 us  [per_device(): pl.pallas_call(kernel, out_shape=(out, out), in_specs=[hbm, hbm, hbm, vme...]
    all_gather x1 -> x0, blocking collectives: 89.4 us -> none  [per_device(): lax.all_gather(head_low, 'dp', axis=0, tiled=True)]
    dot_general x3 -> x0, matrix products: 16.3 us -> none  [the longest x1 14.1 us: per_device(): jnp.dot(weights, piece, preferred_element_type=jnp.float32)]
  transfers between devices with their start and end apart: 2 -> 0, of which waited for: 2 -> 0; matrix products, arithmetic and copies ran while one was open for 0% -> 0% of each run, Pallas kernels for 0% -> 0%
where the time goes in v1:
time: 101 us; the launch traced here: 100 us
  Pallas kernels  93.2 us (92%)
  local copies, waits for them, and re-layouts  6.25 us (6%)
    pallas_call x1, Pallas kernels, per_device(): pl.pallas_call(kernel, out_shape=(out, out), in_specs=[hbm, hbm, hbm, vme...  93.2 us
    unnamed x14, local copies, waits for them, and re-layouts  6.25 us

profile of v1, /device:TPU:6, one launch (start us, length us, event | category | flops | bytes accessed | tf_op | source)
XLA Modules:
  0.0 100.1 jit_solution(2204847618900075031)
XLA Ops:
  0.6 0.0 copy-start.5
  0.6 0.6 copy-done.5
  1.3 0.0 copy-start
  1.3 0.9 copy-done
  2.2 0.0 copy-start.1
  2.2 0.9 copy-done.1
  3.1 0.0 copy-start.2
  3.1 0.9 copy-done.2
  4.1 0.0 copy-start.3
  4.1 0.8 copy-done.3
  4.9 0.0 copy-start.4
  4.9 0.8 copy-done.4
  5.7 93.2 %contrastive_step.1 = (f32[10,768]{1,0:T(8,128)S(1)}, f32[10,768]{1,0:T(8,128)S(1)}) custom-call(bf16[128,768]{1,0:T(8,128)(2,1)S(1)} %bitcast.3, bf16[128,768]{1,0:T(8,128)(2,1)S(1)} %bitcast.4, bf16[128,640]{1,0:T(8,128)(2,1)S(1)} %bitcast.5, f32[10,768]{1,0:T(8,128)S(1)} %copy-done.3, f32[10,768]{1,0:T(8,128)S(1)} %copy-done.4, s32[1,128]{1,0:T(1,128)S(1)} %copy-done.5), custom_call_target="tpu_custom_call" | custom-call | flops 8000000000 | bytes 2000000 | tf_op jit(solution)/shard_map/contrastive_step/pallas_call | solution.py:455
  98.8 0.6 copy.10
  99.5 0.6 copy.11
Async XLA Ops:
  0.6 0.7 copy-start.5
  1.3 0.9 copy-start
  2.2 0.9 copy-start.1
  3.1 0.9 copy-start.2
  4.1 0.8 copy-start.3
  4.9 0.8 copy-start.4

commit v2 on v1

--- a/solution.py
+++ b/solution.py
@@ -24,6 +24,10 @@
 K = 640
 OWN = 10
 PAD = 16
+WIDE = 512
+REST = D - WIDE
+FIRST = 24
+SECOND = 16
 HALF = D // 2
 NT = (((1,), (1,)), ((), ()))
 CHUNKS = 4
@@ -34,12 +38,14 @@
     img_hbm,
     base_hbm,
     feat_hbm,
-    head_ref,
-    momentum_ref,
+    head_hbm,
+    momentum_hbm,
     label_hbm,
     new_head_ref,
     new_momentum_ref,
     img_raw,
+    head_ref,
+    momentum_ref,
     img,
     tb,
     tf,
@@ -57,11 +63,18 @@
     grad_low,
     core_out,
     core_in,
-    x_own,
-    x_out,
-    x_in,
-    y_out,
-    y_in,
+    a_own,
+    a_out,
+    a_in,
+    b_own,
+    b_out,
+    b_in,
+    a2_own,
+    a2_out,
+    a2_in,
+    b2_own,
+    b2_out,
+    b2_in,
     z_out,
     z_in,
     share,
@@ -82,14 +95,14 @@
     hc_recv,
     gc_send,
     gc_recv,
-    gx_send,
-    gx_recv,
-    gy_send,
-    gy_recv,
+    ga_send,
+    ga_recv,
+    gb_send,
+    gb_recv,
     gz_send,
     gz_recv,
-    gb_send,
-    gb_recv,
+    gs_send,
+    gs_recv,
 ):
     dp = lax.axis_index("dp")
     rep = lax.axis_index("replica")
@@ -121,6 +134,8 @@
         pltpu.make_async_copy(base_hbm, tb.at[0], local_sem.at[1]),
         pltpu.make_async_copy(feat_hbm, tf.at[0], local_sem.at[2]),
         pltpu.make_async_copy(label_hbm, tl.at[0], local_sem.at[3]),
+        pltpu.make_async_copy(head_hbm, head_ref, local_sem.at[4]),
+        pltpu.make_async_copy(momentum_hbm, momentum_ref, local_sem.at[5]),
     ]
     for load in loads:
         load.start()
@@ -150,7 +165,10 @@
 
     is_source = (z % 8) == rep
     own_block = head_block(c, x, yl, yh, z // 8)
-    head_low = jnp.concatenate([head_ref[...], jnp.zeros((PAD - OWN, D), F32)], axis=0).astype(BF16)
+    loads[4].wait()
+    left, right = head_ref[:, :WIDE], head_ref[:, WIDE:]
+    right = jnp.concatenate([right[: OWN // 2], right[OWN // 2 :]], axis=1)
+    head_low = jnp.concatenate([left, right, jnp.zeros((1, WIDE), F32)], axis=0).astype(BF16)
 
     @pl.when(is_source)
     def _():
@@ -199,8 +217,8 @@
     for copy in text_c:
         copy.start()
 
-    def ring(s):
-        for k in range(CHUNKS):
+    def ring(s, chunks=range(CHUNKS)):
+        for k in chunks:
             up(s, k).wait_recv()
 
             @pl.when((s < 7) | (k < CHUNKS // 2))
@@ -213,21 +231,38 @@
             def _():
                 dn(s + 1, k).start()
 
+    early, late = range(CHUNKS // 2), range(CHUNKS // 2, CHUNKS)
+
     place = lax.broadcasted_iota(jnp.int32, (1, 64 * PAD), 1)
     block, row = place >> 4, place & 15
     source = ((block >> 3) & 3) + 4 * ((block >> 2) & 1) + 8 * (block & 1)
-    wanted = (source * 4 + ((block >> 1) & 1) * 2 + (block >> 5)) * OWN + row
-    wanted = jnp.where(row < OWN, wanted, -1)
-    pick[...] = (lax.broadcasted_iota(jnp.int32, (K, 64 * PAD), 0) == wanted).astype(F32).astype(BF16)
+    first_row = (source * 4 + ((block >> 1) & 1) * 2 + (block >> 5)) * OWN
+    packed = (row >= OWN) & (row < PAD - 1)
+    row_of = lax.broadcasted_iota(jnp.int32, (K, 64 * PAD), 0)
+    wanted = jnp.where(row < OWN, first_row + row, jnp.where(packed, first_row + row - OWN, -1))
+    pick[0] = (row_of == wanted).astype(F32).astype(BF16)
+    wanted = jnp.where(packed, first_row + row - OWN // 2, -1)
+    pick[1] = (row_of == wanted).astype(F32).astype(BF16)
 
     place = lax.broadcasted_iota(jnp.int32, (K, 1), 0)
     block = (place * 6554) >> 16
-    row = place - block * OWN
     source = ((block >> 4) & 1) * 2 + ((block >> 2) & 1) + 4 * (block & 3)
     owner = source * 4 + ((block >> 3) & 1) * 2 + (c ^ 1 ^ (block >> 5))
-    wanted = owner * OWN + row
+    wanted = owner * OWN + place - block * OWN
     order[...] = (lax.broadcasted_iota(jnp.int32, (K, K), 1) == wanted).astype(F32).astype(BF16)
 
+    def head_y(k):
+        blocks = hb.at[pl.ds(head_block(c, x, yl, yh, 0), 2)]
+        return remote(blocks, blocks, hy_send.at[k], hy_recv.at[k], to_y(k))
+
+    def head_x(k):
+        blocks = hb.at[pl.ds(head_block(c, x, 0, 0, 0), 8)]
+        return remote(blocks, blocks, hx_send.at[k], hx_recv.at[k], to_x(k))
+
+    all_mine = hb.at[pl.ds(c * 32, 32)]
+    head_c = remote(all_mine, all_mine, hc_send, hc_recv, to_core)
+
+    ring(1, early)
     for zh in range(2):
 
         @pl.when(z != rep + 8 * zh)
@@ -235,50 +270,49 @@
             block = hb.at[head_block(c, x, yl, yh, zh)]
             remote(block, block, hz_send.at[0], hz_recv.at[zh], to_z(1)).wait_recv()
 
-    def head_y(k):
-        blocks = hb.at[pl.ds(head_block(c, x, yl, yh, 0), 2)]
-        return remote(blocks, blocks, hy_send.at[k], hy_recv.at[k], to_y(k))
-
-    def head_x(k):
-        blocks = hb.at[pl.ds(head_block(c, x, 0, 0, 0), 8)]
-        return remote(blocks, blocks, hx_send.at[k], hx_recv.at[k], to_x(k))
-
-    all_mine = hb.at[pl.ds(c * 32, 32)]
-    head_c = remote(all_mine, all_mine, hc_send, hc_recv, to_core)
-
     for k in range(1, 4):
         head_y(k).start()
-    ring(1)
+    ring(1, late)
+    ring(2, early)
     for k in range(1, 4):
         head_y(k).wait_recv()
     for k in range(1, 4):
         head_x(k).start()
-    ring(2)
+    ring(2, late)
+    ring(3)
     for copy in text_y:
         copy.wait_recv()
     for copy in text_yc:
         copy.start()
-    for k in range(1, 4):
-        head_x(k).wait_recv()
-    head_c.start()
-    ring(3)
-
-    for load in loads[1:]:
+    ring(4, early)
+
+    for load in loads[1:4]:
         load.wait()
     for copy in text_c + text_yc:
         copy.wait_recv()
     features = tf[...].reshape(4 * ROWS, K)
-    spread[...] = jnp.dot(features, pick[...], preferred_element_type=F32).astype(BF16)
+    whole = jnp.dot(features, pick[0], preferred_element_type=F32)
+    spread[0] = jnp.where(row < OWN, whole, 0.0).astype(BF16)
+    spread[1] = jnp.where(row < OWN, 0.0, whole).astype(BF16)
+    spread[2] = jnp.dot(features, pick[1], preferred_element_type=F32).astype(BF16)
     feat_t[...] = lax.dot_general(order[...], features, NT, preferred_element_type=F32).astype(BF16)
     diagonal = lax.broadcasted_iota(jnp.int32, (ROWS, ROWS), 0) == lax.broadcasted_iota(jnp.int32, (ROWS, ROWS), 1)
     for i in range(4):
         column = jnp.sum(jnp.where(diagonal, tl[i].astype(F32), 0.0), axis=1, keepdims=True)
         label_wide[pl.ds(i * ROWS, ROWS)] = jnp.broadcast_to(column, (ROWS, ROWS)).astype(jnp.int32)
+    ring(4, late)
+    for k in range(1, 4):
+        head_x(k).wait_recv()
+    head_c.start()
+    ring(5, early)
     head_c.wait_recv()
-    head_all = hb[...].reshape(64 * PAD, D)
+    head_all = hb[...].reshape(64 * PAD, WIDE)
     for i in range(4):
         rows = pl.ds(i * ROWS, ROWS)
-        emb = tb[i].astype(F32) + jnp.dot(spread[rows], head_all, preferred_element_type=F32)
+        left = jnp.dot(spread[0, rows], head_all, preferred_element_type=F32)
+        right = jnp.dot(spread[1, rows], head_all[:, :REST], preferred_element_type=F32)
+        right += jnp.dot(spread[2, rows], head_all[:, REST:], preferred_element_type=F32)
+        emb = tb[i].astype(F32) + jnp.concatenate([left, right], axis=1)
         inv = lax.rsqrt(jnp.sum(emb * emb, axis=1, keepdims=True) + norm_epsilon)
         exact = emb * inv
         inv_norm[rows] = inv
@@ -305,11 +339,12 @@
                 unit_grad[rows] += grad
 
     process(img[0], [columns(z)], True)
+    ring(5, late)
 
     def pair(p, carry):
-        @pl.when(p % 2 == 1)
+        @pl.when((p == 3) | (p == 6))
         def _():
-            ring(4 + p // 2)
+            ring(5 + p // 3)
 
         images = img[pl.ds(2 * p - 1, 2)].reshape(2 * ROWS, D)
         process(images, [columns(z - p + NZ), columns(z + p)], False)
@@ -320,6 +355,32 @@
         up(8, k).wait_recv()
         dn(8, k + CHUNKS // 2).wait_recv()
     process(img[15], [columns(z + 8)], False)
+
+    def drain():
+        @pl.when(is_source)
+        def _():
+            def drain_head(k, carry):
+                head_z(k).wait_send()
+                return carry
+
+            lax.fori_loop(1, NZ, drain_head, 0)
+
+        for copy in text_y + text_c + text_yc + [head_c]:
+            copy.wait_send()
+        for k in range(1, 4):
+            head_y(k).wait_send()
+            head_x(k).wait_send()
+
+        def drain_ring(s, carry):
+            for k in range(CHUNKS):
+                up(s, k).wait_send()
+                dn(s, k).wait_send()
+            return carry
+
+        lax.fori_loop(1, 8, drain_ring, 0)
+        for k in range(CHUNKS // 2):
+            up(8, k).wait_send()
+            dn(8, k + CHUNKS // 2).wait_send()
 
     for i in range(4):
         rows = pl.ds(i * ROWS, ROWS)
@@ -337,34 +398,66 @@
         mine = jnp.dot(feat_t[pl.ds(320 + h * 160, 160)], grad_low[...], preferred_element_type=F32)
         to_other(h).wait_recv()
         mine += core_in[h].astype(F32)
+        groups = [mine[k * 40 : (k + 1) * 40] for k in range(4)]
+        first = jnp.concatenate([g[:FIRST] for g in groups], axis=0)
         for side in range(2):
-            part = mine[:, side * HALF : (side + 1) * HALF]
-            x_own[2 * h + side] = part
-            x_out[2 * h + side] = part.astype(BF16)
-
-    def to_x_part(k):
-        return remote(x_out.at[(x + k) % 4], x_in.at[k - 1], gx_send.at[k], gx_recv.at[k], to_x(k))
-
-    for k in range(1, 4):
-        to_x_part(k).start()
-    total = x_own[x]
-    for k in range(1, 4):
-        to_x_part(k).wait_recv()
-        total += x_in[k - 1].astype(F32)
+            part = first[:, side * HALF : (side + 1) * HALF]
+            a_own[2 * h + side] = part
+            a_out[2 * h + side] = part.astype(BF16)
+        for k in range(4):
+            b_own[k, h] = groups[k][FIRST:]
+            b_out[k, h] = groups[k][FIRST:].astype(BF16)
+
+    def a_x(k):
+        return remote(a_out.at[(x + k) % 4], a_in.at[k - 1], ga_send.at[0, k], ga_recv.at[0, k], to_x(k))
+
+    def b_y(k):
+        return remote(b_out.at[(y + k) % 4], b_in.at[k - 1], gb_send.at[0, k], gb_recv.at[0, k], to_y(k))
+
+    def a_y(k):
+        return remote(a2_out.at[(y + k) % 4], a2_in.at[k - 1], ga_send.at[1, k], ga_recv.at[1, k], to_y(k))
+
+    def b_x(k):
+        return remote(b2_out.at[(x + k) % 4], b2_in.at[k - 1], gb_send.at[1, k], gb_recv.at[1, k], to_x(k))
+
+    for k in (2, 1, 3):
+        a_x(k).start()
+        b_y(k).start()
+    drain()
+    total = b_own[y]
+    for k in (1, 3, 2):
+        b_y(k).wait_recv()
+        total += b_in[k - 1].astype(F32)
+    for h in range(2):
+        for side in range(2):
+            part = total[h, :, side * HALF : (side + 1) * HALF]
+            b2_own[2 * h + side] = part
+            b2_out[2 * h + side] = part.astype(BF16)
+    for k in (2, 1, 3):
+        b_x(k).start()
+    total = a_own[x]
+    for k in (1, 3, 2):
+        a_x(k).wait_recv()
+        total += a_in[k - 1].astype(F32)
     for k in range(4):
-        y_out[k] = total[k * 40 : (k + 1) * 40]
-
-    def to_y_part(k):
-        return remote(y_out.at[(y + k) % 4], y_in.at[k - 1], gy_send.at[k], gy_recv.at[k], to_y(k))
-
-    for k in range(1, 4):
-        to_y_part(k).start()
-    total = y_out[y]
-    for k in range(1, 4):
-        to_y_part(k).wait_recv()
-        total += y_in[k - 1]
+        part = total[k * FIRST : (k + 1) * FIRST]
+        a2_own[k] = part
+        a2_out[k] = jnp.concatenate([part, jnp.zeros((32 - FIRST, HALF), F32)], axis=0).astype(BF16)
+    for k in (2, 1, 3):
+        a_y(k).start()
+    second = b2_own[x]
+    for k in (1, 3, 2):
+        b_x(k).wait_recv()
+        second += b2_in[k - 1].astype(F32)
+    first = a2_own[y]
+    for k in (1, 3, 2):
+        a_y(k).wait_recv()
+        first += a2_in[k - 1, :FIRST].astype(F32)
+    total = jnp.concatenate([first, second], axis=0)
     for j in range(4):
-        z_out[j] = jnp.concatenate([total[j * OWN : (j + 1) * OWN], jnp.zeros((PAD - OWN, HALF), F32)], axis=0)
+        part = total[j * OWN : (j + 1) * OWN]
+        thirds = [part[:, i * 128 : (i + 1) * 128] for i in range(3)] + [jnp.zeros((2, 128), F32)]
+        z_out[j] = jnp.concatenate(thirds, axis=0).astype(BF16)
 
     group = 2 * (x // 2) + yl
 
@@ -384,14 +477,14 @@
     def to_share(i):
         rep2 = (rep + i) % 8
         device = (dp, rep2)
-        return remote(share.at[side], share.at[side], gb_send.at[i], gb_recv.at[side], device)
+        return remote(share.at[side], share.at[side], gs_send.at[i], gs_recv.at[side], device)
 
     @pl.when(is_owner)
     def _():
         z_in[0] = z_out[z // 4]
         for k in range(1, NZ):
             remote(z_out.at[0], z_in.at[k], gz_send.at[0], gz_recv.at[k], to_z(1)).wait_recv()
-        share[side] = jnp.sum(z_in[...], axis=0)
+        share[side] = jnp.sum(z_in[...].astype(F32), axis=0)
         for i in range(1, 8):
             to_share(i).start()
 
@@ -399,39 +492,20 @@
 
         @pl.when(jnp.logical_not(is_owner & (side == s)))
         def _():
-            remote(share.at[s], share.at[s], gb_send.at[0], gb_recv.at[s], to_x(1)).wait_recv()
-
-    head_grad = jnp.concatenate([share[0, :OWN], share[1, :OWN]], axis=1) * (1.0 / 8.0)
+            remote(share.at[s], share.at[s], gs_send.at[0], gs_recv.at[s], to_x(1)).wait_recv()
+
+    pieces = [share[s, i * OWN : (i + 1) * OWN] for s in range(2) for i in range(3)]
+    head_grad = jnp.concatenate(pieces, axis=1) * (1.0 / 8.0)
+    loads[5].wait()
     momentum = momentum_decay * momentum_ref[...] + (1.0 - momentum_decay) * head_grad
     new_momentum_ref[...] = momentum
     new_head_ref[...] = head_ref[...] - outer_rate * ((1.0 - blend_weight) * head_grad + blend_weight * momentum)
 
-    @pl.when(is_source)
-    def _():
-        def drain(k, carry):
-            head_z(k).wait_send()
-            return carry
-
-        lax.fori_loop(1, NZ, drain, 0)
-
-    for copy in text_y + text_c + text_yc + [head_c]:
-        copy.wait_send()
-
-    def drain_ring(s, carry):
-        for k in range(CHUNKS):
-            up(s, k).wait_send()
-            dn(s, k).wait_send()
-        return carry
-
-    lax.fori_loop(1, 8, drain_ring, 0)
-    for k in range(CHUNKS // 2):
-        up(8, k).wait_send()
-        dn(8, k + CHUNKS // 2).wait_send()
     for k in range(1, 4):
-        head_y(k).wait_send()
-        head_x(k).wait_send()
-        to_x_part(k).wait_send()
-        to_y_part(k).wait_send()
+        a_x(k).wait_send()
+        b_y(k).wait_send()
+        a_y(k).wait_send()
+        b_x(k).wait_send()
     for h in range(2):
         to_other(h).wait_send()
     for j in range(4):
@@ -455,18 +529,20 @@
     return pl.pallas_call(
         kernel,
         out_shape=(out, out),
-        in_specs=[hbm, hbm, hbm, vmem, vmem, hbm],
+        in_specs=[hbm] * 6,
         out_specs=(vmem, vmem),
         scratch_shapes=[
             pltpu.VMEM((ROWS, D), BF16),
+            pltpu.VMEM((OWN, D), F32),
+            pltpu.VMEM((OWN, D), F32),
             pltpu.VMEM((NZ, ROWS, D), BF16),
             pltpu.VMEM((4, ROWS, D), BF16),
             pltpu.VMEM((4, ROWS, K), BF16),
             pltpu.VMEM((4, 1, ROWS), jnp.int32),
-            pltpu.VMEM((64, PAD, D), BF16),
-            pltpu.VMEM((K, 64 * PAD), BF16),
+            pltpu.VMEM((64, PAD, WIDE), BF16),
+            pltpu.VMEM((2, K, 64 * PAD), BF16),
             pltpu.VMEM((K, K), BF16),
-            pltpu.VMEM((texts, 64 * PAD), BF16),
+            pltpu.VMEM((3, texts, 64 * PAD), BF16),
             pltpu.VMEM((K, texts), BF16),
             pltpu.VMEM((texts, D), F32),
             pltpu.VMEM((texts, D), BF16),
@@ -476,15 +552,22 @@
             pltpu.VMEM((texts, D), BF16),
             pltpu.VMEM((2, 160, D), BF16),
             pltpu.VMEM((2, 160, D), BF16),
-            pltpu.VMEM((4, 160, HALF), F32),
-            pltpu.VMEM((4, 160, HALF), BF16),
-            pltpu.VMEM((3, 160, HALF), BF16),
-            pltpu.VMEM((4, 40, HALF), F32),
-            pltpu.VMEM((3, 40, HALF), F32),
-            pltpu.VMEM((4, PAD, HALF), F32),
-            pltpu.VMEM((NZ, PAD, HALF), F32),
-            pltpu.VMEM((2, PAD, HALF), F32),
-            dma((4,)),
+            pltpu.VMEM((4, 4 * FIRST, HALF), F32),
+            pltpu.VMEM((4, 4 * FIRST, HALF), BF16),
+            pltpu.VMEM((3, 4 * FIRST, HALF), BF16),
+            pltpu.VMEM((4, 2, SECOND, D), F32),
+            pltpu.VMEM((4, 2, SECOND, D), BF16),
+            pltpu.VMEM((3, 2, SECOND, D), BF16),
+            pltpu.VMEM((4, FIRST, HALF), F32),
+            pltpu.VMEM((4, 32, HALF), BF16),
+            pltpu.VMEM((3, 32, HALF), BF16),
+            pltpu.VMEM((4, SECOND, HALF), F32),
+            pltpu.VMEM((4, SECOND, HALF), BF16),
+            pltpu.VMEM((3, SECOND, HALF), BF16),
+            pltpu.VMEM((4, 32, 128), BF16),
+            pltpu.VMEM((NZ, 32, 128), BF16),
+            pltpu.VMEM((2, 32, 128), F32),
+            dma((6,)),
             dma((9, CHUNKS)),
             dma((9, CHUNKS)),
             dma((9, CHUNKS)),
@@ -501,17 +584,17 @@
             dma,
             dma((2,)),
             dma((2,)),
-            dma((4,)),
-            dma((4,)),
-            dma((4,)),
-            dma((4,)),
+            dma((2, 4)),
+            dma((2, 4)),
+            dma((2, 4)),
+            dma((2, 4)),
             dma((4,)),
             dma((NZ,)),
             dma((8,)),
             dma((2,)),
         ],
         compiler_params=pltpu.CompilerParams(
-            collective_id=0, has_side_effects=True, vmem_limit_bytes=48 * 1024 * 1024
+            collective_id=0, has_side_effects=True, vmem_limit_bytes=63 * 1024 * 1024
         ),
         cost_estimate=pl.CostEstimate(flops=8_000_000_000, bytes_accessed=2_000_000, transcendentals=1_100_000),
         name="contrastive_step",

time: 101 us -> 83.4 us (0.83)
  Pallas kernels: 93.2 us -> 80.2 us
  local copies, waits for them, and re-layouts: 6.25 us -> 2.06 us
    pallas_call x1, Pallas kernels: 93.2 us -> 80.2 us  [per_device(): pl.pallas_call(kernel, out_shape=(out, out), in_specs=[hbm] * 6, out_spec...]
    unnamed x14 -> x4, local copies, waits for them, and re-layouts: 6.25 us -> 2.06 us
where the time goes in v2:
time: 83.4 us; the launch traced here: 82.9 us
  Pallas kernels  80.2 us (96%)
  local copies, waits for them, and re-layouts  2.06 us (2%)
    pallas_call x1, Pallas kernels, per_device(): pl.pallas_call(kernel, out_shape=(out, out), in_specs=[hbm] * 6, out_spec...  80.2 us
    unnamed x4, local copies, waits for them, and re-layouts  2.06 us

profile of v2, /device:TPU:6, one launch (start us, length us, event | category | flops | bytes accessed | tf_op | source)
XLA Modules:
  0.0 82.9 jit_solution(18167722003889789298)
XLA Ops:
  0.6 80.2 %contrastive_step.1 = (f32[10,768]{1,0:T(8,128)}, f32[10,768]{1,0:T(8,128)}) custom-call(bf16[128,768]{1,0:T(8,128)(2,1)} %bitcast.3, bf16[128,768]{1,0:T(8,128)(2,1)} %bitcast.4, bf16[128,640]{1,0:T(8,128)(2,1)} %bitcast.5, f32[10,768]{1,0:T(8,128)} %head_hbm.1, f32[10,768]{1,0:T(8,128)} %momentum_hbm.1, s32[1,128]{1,0:T(1,128)} %label_hbm.1), custom_call_target="tpu_custom_call" | custom-call | flops 8000000000 | bytes 2000000 | tf_op jit(solution)/shard_map/contrastive_step/pallas_call | solution.py:529
  80.8 0.0 copy-start
  80.8 1.4 %copy.10 = f32[10,768]{1,0:T(8,128)} copy(f32[10,768]{1,0:T(8,128)} %get-tuple-element.4) | data formatting | bytes 61440
  82.3 0.0 copy-done
  82.3 0.6 copy.11
Async XLA Ops:
  80.8 1.4 %copy-start = (f32[10,768]{1,0:T(8,128)S(1)}, f32[10,768]{1,0:T(8,128)}, u32[]{:S(2)}) copy-start(f32[10,768]{1,0:T(8,128)} %get-tuple-element.5) | copy-start | bytes 92164

commit v3 on v2

--- a/solution.py
+++ b/solution.py
@@ -39,13 +39,10 @@
     base_hbm,
     feat_hbm,
     head_hbm,
-    momentum_hbm,
     label_hbm,
-    new_head_ref,
-    new_momentum_ref,
+    head_grad_ref,
     img_raw,
     head_ref,
-    momentum_ref,
     img,
     tb,
     tf,
@@ -61,8 +58,8 @@
     label_wide,
     unit_grad,
     grad_low,
-    core_out,
-    core_in,
+    grad_in,
+    partial,
     a_own,
     a_out,
     a_in,
@@ -135,7 +132,6 @@
         pltpu.make_async_copy(feat_hbm, tf.at[0], local_sem.at[2]),
         pltpu.make_async_copy(label_hbm, tl.at[0], local_sem.at[3]),
         pltpu.make_async_copy(head_hbm, head_ref, local_sem.at[4]),
-        pltpu.make_async_copy(momentum_hbm, momentum_ref, local_sem.at[5]),
     ]
     for load in loads:
         load.start()
@@ -145,16 +141,21 @@
     def greet(device):
         pl.semaphore_signal(barrier, inc=1, device_id=device, device_id_type=MESH)
 
-    def greet_z(k, carry):
-        greet(to_z(k))
-        return carry
-
-    lax.fori_loop(1, NZ, greet_z, 0)
+    head_z0 = (rep + 4 * c) % 8
+    is_source = (z % 8) == head_z0
+    greet(to_z(1))
+    greet(to_z(NZ - 1))
     greet(to_core)
     for k in range(1, 4):
         greet(to_x(k))
         greet(to_y(k))
         greet(at(z, yh * 2 + (1 - yl), (x + k) % 4, c))
+    for zh in range(2):
+        away = (head_z0 + 8 * zh - z + NZ) % NZ
+
+        @pl.when((away > 1) & (away < NZ - 1))
+        def _():
+            greet(to_z(away))
 
     loads[0].wait()
     wide = img_raw[...].astype(F32)
@@ -163,7 +164,6 @@
     def head_block(c2, x2, yl2, yh2, zh2):
         return (((c2 * 4 + x2) * 2 + yl2) * 2 + yh2) * 2 + zh2
 
-    is_source = (z % 8) == rep
     own_block = head_block(c, x, yl, yh, z // 8)
     loads[4].wait()
     left, right = head_ref[:, :WIDE], head_ref[:, WIDE:]
@@ -174,7 +174,7 @@
     def _():
         hb[own_block] = head_low
 
-    pl.semaphore_wait(barrier, 15 + 1 + 9)
+    pl.semaphore_wait(barrier, jnp.where(is_source, 15 + 1 + 9, 2 + 1 + 9))
 
     def head_z(k):
         block = hb.at[own_block]
@@ -235,7 +235,7 @@
 
     place = lax.broadcasted_iota(jnp.int32, (1, 64 * PAD), 1)
     block, row = place >> 4, place & 15
-    source = ((block >> 3) & 3) + 4 * ((block >> 2) & 1) + 8 * (block & 1)
+    source = ((block >> 3) & 3) + 4 * (((block >> 2) ^ (block >> 5)) & 1) + 8 * (block & 1)
     first_row = (source * 4 + ((block >> 1) & 1) * 2 + (block >> 5)) * OWN
     packed = (row >= OWN) & (row < PAD - 1)
     row_of = lax.broadcasted_iota(jnp.int32, (K, 64 * PAD), 0)
@@ -244,12 +244,12 @@
     wanted = jnp.where(packed, first_row + row - OWN // 2, -1)
     pick[1] = (row_of == wanted).astype(F32).astype(BF16)
 
-    place = lax.broadcasted_iota(jnp.int32, (K, 1), 0)
+    place = lax.broadcasted_iota(jnp.int32, (K // 2, 1), 0)
     block = (place * 6554) >> 16
     source = ((block >> 4) & 1) * 2 + ((block >> 2) & 1) + 4 * (block & 3)
-    owner = source * 4 + ((block >> 3) & 1) * 2 + (c ^ 1 ^ (block >> 5))
+    owner = source * 4 + ((block >> 3) & 1) * 2 + c
     wanted = owner * OWN + place - block * OWN
-    order[...] = (lax.broadcasted_iota(jnp.int32, (K, K), 1) == wanted).astype(F32).astype(BF16)
+    order[...] = (lax.broadcasted_iota(jnp.int32, (K // 2, K), 1) == wanted).astype(F32).astype(BF16)
 
     def head_y(k):
         blocks = hb.at[pl.ds(head_block(c, x, yl, yh, 0), 2)]
@@ -262,29 +262,28 @@
     all_mine = hb.at[pl.ds(c * 32, 32)]
     head_c = remote(all_mine, all_mine, hc_send, hc_recv, to_core)
 
-    ring(1, early)
+    ring(1)
     for zh in range(2):
 
-        @pl.when(z != rep + 8 * zh)
+        @pl.when(z != head_z0 + 8 * zh)
         def _():
             block = hb.at[head_block(c, x, yl, yh, zh)]
             remote(block, block, hz_send.at[0], hz_recv.at[zh], to_z(1)).wait_recv()
 
     for k in range(1, 4):
         head_y(k).start()
-    ring(1, late)
-    ring(2, early)
+    ring(2)
     for k in range(1, 4):
         head_y(k).wait_recv()
-    for k in range(1, 4):
+    for k in (2, 1, 3):
         head_x(k).start()
-    ring(2, late)
     ring(3)
+    ring(4, early)
     for copy in text_y:
         copy.wait_recv()
     for copy in text_yc:
         copy.start()
-    ring(4, early)
+    ring(4, late)
 
     for load in loads[1:4]:
         load.wait()
@@ -300,11 +299,11 @@
     for i in range(4):
         column = jnp.sum(jnp.where(diagonal, tl[i].astype(F32), 0.0), axis=1, keepdims=True)
         label_wide[pl.ds(i * ROWS, ROWS)] = jnp.broadcast_to(column, (ROWS, ROWS)).astype(jnp.int32)
-    ring(4, late)
+    ring(5)
     for k in range(1, 4):
         head_x(k).wait_recv()
     head_c.start()
-    ring(5, early)
+    ring(6, early)
     head_c.wait_recv()
     head_all = hb[...].reshape(64 * PAD, WIDE)
     for i in range(4):
@@ -324,13 +323,14 @@
     def columns(z2):
         return ((z2 % NZ) * 4 + yh * 2 + c) * ROWS + lane
 
-    def process(images, marks, fresh):
-        for i in range(2):
-            rows = pl.ds(i * 256, 256)
-            raw = lax.dot_general(text_unit[rows], images, NT, preferred_element_type=F32)
+    def process(first, blocks, marks, fresh=False):
+        images = img[pl.ds(first, blocks)].reshape(blocks * ROWS, D)
+        halves = [pl.ds(i * 256, 256) for i in range(2)]
+        raws = [lax.dot_general(text_unit[rows], images, NT, preferred_element_type=F32) for rows in halves]
+        for rows, raw in zip(halves, raws):
             chance = 0.5 * jnp.tanh((0.5 * logit_scale) * raw + 0.5 * logit_bias) + 0.5
             labels = label_wide[rows]
-            match = jnp.concatenate([(labels == m) for m in marks], axis=1)
+            match = jnp.concatenate([(labels == columns(z + m + NZ)) for m in marks], axis=1)
             weights = jnp.where(match, chance - 1.0, chance).astype(BF16)
             grad = jnp.dot(weights, images, preferred_element_type=F32)
             if fresh:
@@ -338,23 +338,17 @@
             else:
                 unit_grad[rows] += grad
 
-    process(img[0], [columns(z)], True)
-    ring(5, late)
-
-    def pair(p, carry):
-        @pl.when((p == 3) | (p == 6))
-        def _():
-            ring(5 + p // 3)
-
-        images = img[pl.ds(2 * p - 1, 2)].reshape(2 * ROWS, D)
-        process(images, [columns(z - p + NZ), columns(z + p)], False)
-        return carry
-
-    lax.fori_loop(1, 8, pair, 0)
+    ring(6, late)
+    process(0, 4, (0, -1, 1, -2), True)
+    ring(7, early)
+    process(4, 4, (2, -3, 3, -4))
+    ring(7, late)
+    process(8, 4, (4, -5, 5, -6))
+    process(12, 3, (6, -7, 7))
     for k in range(CHUNKS // 2):
         up(8, k).wait_recv()
         dn(8, k + CHUNKS // 2).wait_recv()
-    process(img[15], [columns(z + 8)], False)
+    process(15, 1, (8,))
 
     def drain():
         @pl.when(is_source)
@@ -382,52 +376,61 @@
             up(8, k).wait_send()
             dn(8, k + CHUNKS // 2).wait_send()
 
+    def to_other(i):
+        rows, there = pl.ds(i * ROWS, ROWS), pl.ds((i ^ 1) * ROWS, ROWS)
+        return remote(grad_low.at[rows], grad_in.at[there], gc_send.at[i], gc_recv.at[i], to_core)
+
     for i in range(4):
         rows = pl.ds(i * ROWS, ROWS)
         exact, grad = text_exact[rows], unit_grad[rows]
         along = jnp.sum(exact * grad, axis=1, keepdims=True)
         grad_low[rows] = ((grad - exact * along) * (logit_scale * inv_norm[rows])).astype(BF16)
-
-    def to_other(h):
-        return remote(core_out.at[h], core_in.at[h], gc_send.at[h], gc_recv.at[h], to_core)
+        to_other(i).start()
+
+    def a_x(k):
+        return remote(a_out.at[(x + k) % 4], a_in.at[k - 1], ga_send.at[0, k], ga_recv.at[0], to_x(k))
+
+    def b_y(k):
+        return remote(b_out.at[(y + k) % 4], b_in.at[k - 1], gb_send.at[0, k], gb_recv.at[0], to_y(k))
+
+    def a_y(k):
+        return remote(a2_out.at[(y + k) % 4], a2_in.at[k - 1], ga_send.at[1, k], ga_recv.at[1], to_y(k))
+
+    def b_x(k):
+        return remote(b2_out.at[(x + k) % 4], b2_in.at[k - 1], gb_send.at[1, k], gb_recv.at[1], to_x(k))
+
+    def all_in(ref, sem):
+        remote(ref, ref, ga_send.at[0, 0], sem, to_x(1)).wait_recv()
 
     for h in range(2):
-        core_out[h] = jnp.dot(feat_t[pl.ds(h * 160, 160)], grad_low[...], preferred_element_type=F32).astype(BF16)
-        to_other(h).start()
+        partial[h] = jnp.dot(feat_t[pl.ds(h * 160, 160)], grad_low[...], preferred_element_type=F32)
+    for i in range(4):
+        to_other(i).wait_recv()
     for h in range(2):
-        mine = jnp.dot(feat_t[pl.ds(320 + h * 160, 160)], grad_low[...], preferred_element_type=F32)
-        to_other(h).wait_recv()
-        mine += core_in[h].astype(F32)
+        mine = partial[h] + jnp.dot(feat_t[pl.ds(h * 160, 160)], grad_in[...], preferred_element_type=F32)
         groups = [mine[k * 40 : (k + 1) * 40] for k in range(4)]
         first = jnp.concatenate([g[:FIRST] for g in groups], axis=0)
         for side in range(2):
             part = first[:, side * HALF : (side + 1) * HALF]
             a_own[2 * h + side] = part
             a_out[2 * h + side] = part.astype(BF16)
+        for k in (2, 1, 3):
+
+            @pl.when((x + k) % 4 // 2 == h)
+            def _():
+                a_x(k).start()
+
         for k in range(4):
             b_own[k, h] = groups[k][FIRST:]
             b_out[k, h] = groups[k][FIRST:].astype(BF16)
 
-    def a_x(k):
-        return remote(a_out.at[(x + k) % 4], a_in.at[k - 1], ga_send.at[0, k], ga_recv.at[0, k], to_x(k))
-
-    def b_y(k):
-        return remote(b_out.at[(y + k) % 4], b_in.at[k - 1], gb_send.at[0, k], gb_recv.at[0, k], to_y(k))
-
-    def a_y(k):
-        return remote(a2_out.at[(y + k) % 4], a2_in.at[k - 1], ga_send.at[1, k], ga_recv.at[1, k], to_y(k))
-
-    def b_x(k):
-        return remote(b2_out.at[(x + k) % 4], b2_in.at[k - 1], gb_send.at[1, k], gb_recv.at[1, k], to_x(k))
-
     for k in (2, 1, 3):
-        a_x(k).start()
         b_y(k).start()
     drain()
+    all_in(b_in, gb_recv.at[0])
     total = b_own[y]
-    for k in (1, 3, 2):
-        b_y(k).wait_recv()
-        total += b_in[k - 1].astype(F32)
+    for k in range(3):
+        total += b_in[k].astype(F32)
     for h in range(2):
         for side in range(2):
             part = total[h, :, side * HALF : (side + 1) * HALF]
@@ -435,24 +438,24 @@
             b2_out[2 * h + side] = part.astype(BF16)
     for k in (2, 1, 3):
         b_x(k).start()
+    all_in(a_in, ga_recv.at[0])
     total = a_own[x]
-    for k in (1, 3, 2):
-        a_x(k).wait_recv()
-        total += a_in[k - 1].astype(F32)
+    for k in range(3):
+        total += a_in[k].astype(F32)
     for k in range(4):
         part = total[k * FIRST : (k + 1) * FIRST]
         a2_own[k] = part
         a2_out[k] = jnp.concatenate([part, jnp.zeros((32 - FIRST, HALF), F32)], axis=0).astype(BF16)
     for k in (2, 1, 3):
         a_y(k).start()
+    all_in(b2_in, gb_recv.at[1])
     second = b2_own[x]
-    for k in (1, 3, 2):
-        b_x(k).wait_recv()
-        second += b2_in[k - 1].astype(F32)
+    for k in range(3):
+        second += b2_in[k].astype(F32)
+    all_in(a2_in, ga_recv.at[1])
     first = a2_own[y]
-    for k in (1, 3, 2):
-        a_y(k).wait_recv()
-        first += a2_in[k - 1, :FIRST].astype(F32)
+    for k in range(3):
+        first += a2_in[k, :FIRST].astype(F32)
     total = jnp.concatenate([first, second], axis=0)
     for j in range(4):
         part = total[j * OWN : (j + 1) * OWN]
@@ -463,7 +466,7 @@
 
     def to_z_part(j):
         k = (group + 4 * j - z + NZ) % NZ
-        return remote(z_out.at[j], z_in.at[k], gz_send.at[j], gz_recv.at[k], to_z(k))
+        return remote(z_out.at[j], z_in.at[k], gz_send.at[j], gz_recv, to_z(k))
 
     for j in range(4):
 
@@ -482,8 +485,8 @@
     @pl.when(is_owner)
     def _():
         z_in[0] = z_out[z // 4]
-        for k in range(1, NZ):
-            remote(z_out.at[0], z_in.at[k], gz_send.at[0], gz_recv.at[k], to_z(1)).wait_recv()
+        others = z_in.at[pl.ds(1, NZ - 1)]
+        remote(others, others, gz_send.at[0], gz_recv, to_z(1)).wait_recv()
         share[side] = jnp.sum(z_in[...].astype(F32), axis=0)
         for i in range(1, 8):
             to_share(i).start()
@@ -495,19 +498,15 @@
             remote(share.at[s], share.at[s], gs_send.at[0], gs_recv.at[s], to_x(1)).wait_recv()
 
     pieces = [share[s, i * OWN : (i + 1) * OWN] for s in range(2) for i in range(3)]
-    head_grad = jnp.concatenate(pieces, axis=1) * (1.0 / 8.0)
-    loads[5].wait()
-    momentum = momentum_decay * momentum_ref[...] + (1.0 - momentum_decay) * head_grad
-    new_momentum_ref[...] = momentum
-    new_head_ref[...] = head_ref[...] - outer_rate * ((1.0 - blend_weight) * head_grad + blend_weight * momentum)
+    head_grad_ref[...] = jnp.concatenate(pieces, axis=1) * (1.0 / 8.0)
 
     for k in range(1, 4):
         a_x(k).wait_send()
         b_y(k).wait_send()
         a_y(k).wait_send()
         b_x(k).wait_send()
-    for h in range(2):
-        to_other(h).wait_send()
+    for i in range(4):
+        to_other(i).wait_send()
     for j in range(4):
 
         @pl.when(z != group + 4 * j)
@@ -526,14 +525,13 @@
     dma = pltpu.SemaphoreType.DMA
     texts = 4 * ROWS
     out = jax.ShapeDtypeStruct((OWN, D), F32)
-    return pl.pallas_call(
+    head_grad = pl.pallas_call(
         kernel,
-        out_shape=(out, out),
-        in_specs=[hbm] * 6,
-        out_specs=(vmem, vmem),
+        out_shape=out,
+        in_specs=[hbm] * 5,
+        out_specs=vmem,
         scratch_shapes=[
             pltpu.VMEM((ROWS, D), BF16),
-            pltpu.VMEM((OWN, D), F32),
             pltpu.VMEM((OWN, D), F32),
             pltpu.VMEM((NZ, ROWS, D), BF16),
             pltpu.VMEM((4, ROWS, D), BF16),
@@ -541,17 +539,17 @@
             pltpu.VMEM((4, 1, ROWS), jnp.int32),
             pltpu.VMEM((64, PAD, WIDE), BF16),
             pltpu.VMEM((2, K, 64 * PAD), BF16),
-            pltpu.VMEM((K, K), BF16),
+            pltpu.VMEM((K // 2, K), BF16),
             pltpu.VMEM((3, texts, 64 * PAD), BF16),
-            pltpu.VMEM((K, texts), BF16),
+            pltpu.VMEM((K // 2, texts), BF16),
             pltpu.VMEM((texts, D), F32),
             pltpu.VMEM((texts, D), BF16),
             pltpu.VMEM((texts, 1), F32),
             pltpu.VMEM((texts, ROWS), jnp.int32),
             pltpu.VMEM((texts, D), F32),
             pltpu.VMEM((texts, D), BF16),
-            pltpu.VMEM((2, 160, D), BF16),
-            pltpu.VMEM((2, 160, D), BF16),
+            pltpu.VMEM((texts, D), BF16),
+            pltpu.VMEM((2, 160, D), F32),
             pltpu.VMEM((4, 4 * FIRST, HALF), F32),
             pltpu.VMEM((4, 4 * FIRST, HALF), BF16),
             pltpu.VMEM((3, 4 * FIRST, HALF), BF16),
@@ -567,7 +565,7 @@
             pltpu.VMEM((4, 32, 128), BF16),
             pltpu.VMEM((NZ, 32, 128), BF16),
             pltpu.VMEM((2, 32, 128), F32),
-            dma((6,)),
+            dma((5,)),
             dma((9, CHUNKS)),
             dma((9, CHUNKS)),
             dma((9, CHUNKS)),
@@ -582,14 +580,14 @@
             dma((4,)),
             dma,
             dma,
-            dma((2,)),
+            dma((4,)),
+            dma((4,)),
+            dma((2, 4)),
             dma((2,)),
             dma((2, 4)),
-            dma((2, 4)),
-            dma((2, 4)),
-            dma((2, 4)),
+            dma((2,)),
             dma((4,)),
-            dma((NZ,)),
+            dma,
             dma((8,)),
             dma((2,)),
         ],
@@ -598,7 +596,10 @@
         ),
         cost_estimate=pl.CostEstimate(flops=8_000_000_000, bytes_accessed=2_000_000, transcendentals=1_100_000),
         name="contrastive_step",
-    )(img_emb[0], txt_base[0], txt_feat[0], head, momentum, positive_image)
+    )(img_emb[0], txt_base[0], txt_feat[0], head, positive_image)
+    new_momentum = momentum_decay * momentum + (1.0 - momentum_decay) * head_grad
+    new_head = head - outer_rate * ((1.0 - blend_weight) * head_grad + blend_weight * new_momentum)
+    return (new_head, new_momentum)
 
 
 def solution(mesh):

time: 83.4 us -> 80 us (0.959)
  Pallas kernels: 80.2 us -> 77.4 us
  local copies, waits for them, and re-layouts: 2.06 us -> 0.01 us
  other arithmetic: 0 us -> 1.45 us
    pallas_call x1, Pallas kernels: 80.2 us -> 77.4 us  [per_device(): pl.pallas_call(kernel, out_shape=out, in_specs=[hbm] * 5, out_specs=vmem,...]
    unnamed x4, local copies, waits for them, and re-layouts: 2.06 us -> 0.01 us
    sub x0 -> x1, other arithmetic: none -> 1.45 us  [per_device(): head - outer_rate * ((1.0 - blend_weight) * head_grad + blend_weight * ne...]
where the time goes in v3:
time: 80 us; the launch traced here: 79.5 us
  Pallas kernels  77.4 us (97%)
  other arithmetic  1.45 us (2%)
    pallas_call x1, Pallas kernels, per_device(): pl.pallas_call(kernel, out_shape=out, in_specs=[hbm] * 5, out_specs=vmem,...  77.4 us

profile of v3, /device:TPU:6, one launch (start us, length us, event | category | flops | bytes accessed | tf_op | source)
XLA Modules:
  0.0 79.5 jit_solution(1242153222647143115)
XLA Ops:
  0.6 0.0 copy-start
  0.6 0.0 copy-start.1
  0.7 77.4 %contrastive_step.1 = f32[10,768]{1,0:T(8,128)} custom-call(bf16[128,768]{1,0:T(8,128)(2,1)} %bitcast.3, bf16[128,768]{1,0:T(8,128)(2,1)} %bitcast.4, bf16[128,640]{1,0:T(8,128)(2,1)} %bitcast.5, f32[10,768]{1,0:T(8,128)} %head_hbm.1, s32[1,128]{1,0:T(1,128)} %label_hbm.1), custom_call_target="tpu_custom_call" | custom-call | flops 8000000000 | bytes 2000000 | tf_op jit(solution)/shard_map/contrastive_step/pallas_call | solution.py:528
  78.0 0.0 copy-done
  78.1 0.0 copy-done.1
  78.1 1.4 %multiply_subtract_fusion = (f32[10,768]{1,0:T(8,128)}, f32[10,768]{1,0:T(8,128)}) fusion(f32[10,768]{1,0:T(8,128)S(1)} %copy-done, f32[10,768]{1,0:T(8,128)} %contrastive_step.1, f32[10,768]{1,0:T(8,128)S(1)} %copy-done.1), kind=kLoop, calls=%fused_computation | loop fusion | flops 61440 | bytes 153600 | tf_op jit(solution)/shard_map/sub | solution.py:601
Async XLA Ops:
  0.6 77.4 %copy-start = (f32[10,768]{1,0:T(8,128)S(1)}, f32[10,768]{1,0:T(8,128)}, u32[]{:S(2)}) copy-start(f32[10,768]{1,0:T(8,128)} %head_hbm.1) | copy-start | bytes 92164
  0.6 77.4 %copy-start.1 = (f32[10,768]{1,0:T(8,128)S(1)}, f32[10,768]{1,0:T(8,128)}, u32[]{:S(2)}) copy-start(f32[10,768]{1,0:T(8,128)} %param.10) | copy-start | bytes 92164

commit v4 on v3

--- a/solution.py
+++ b/solution.py
@@ -60,18 +60,23 @@
     grad_low,
     grad_in,
     partial,
-    a_own,
-    a_out,
-    a_in,
-    b_own,
-    b_out,
-    b_in,
-    a2_own,
-    a2_out,
-    a2_in,
-    b2_own,
-    b2_out,
-    b2_in,
+    piece,
+    x_out,
+    x_in,
+    x_far_out,
+    x_far_in,
+    y_out,
+    y_in,
+    y_far_out,
+    y_far_in,
+    x2_out,
+    x2_in,
+    x2_far_out,
+    x2_far_in,
+    y2_out,
+    y2_in,
+    y2_far_out,
+    y2_far_in,
     z_out,
     z_in,
     share,
@@ -198,8 +203,6 @@
     text_y = text_copies(own_text, 2, to_y(2), 0)
     text_c = text_copies(own_text, 1, to_core, 3)
     text_yc = text_copies((tb.at[2], tf.at[2], tl.at[2]), 3, to_core, 6)
-    for copy in text_y:
-        copy.start()
 
     def up(s, k):
         rows = pl.ds(k * PIECE, PIECE)
@@ -216,6 +219,8 @@
         dn(1, k).start()
     for copy in text_c:
         copy.start()
+    text_y[0].start()
+    text_y[2].start()
 
     def ring(s, chunks=range(CHUNKS)):
         for k in chunks:
@@ -230,6 +235,10 @@
             @pl.when((s < 7) | (k >= CHUNKS // 2))
             def _():
                 dn(s + 1, k).start()
+
+            if s > 1:
+                up(s - 1, k).wait_send()
+                dn(s - 1, k).wait_send()
 
     early, late = range(CHUNKS // 2), range(CHUNKS // 2, CHUNKS)
 
@@ -241,28 +250,28 @@
     row_of = lax.broadcasted_iota(jnp.int32, (K, 64 * PAD), 0)
     wanted = jnp.where(row < OWN, first_row + row, jnp.where(packed, first_row + row - OWN, -1))
     pick[0] = (row_of == wanted).astype(F32).astype(BF16)
+    def head_y(k):
+        blocks = hb.at[pl.ds(head_block(c, x, yl, yh, 0), 2)]
+        return remote(blocks, blocks, hy_send.at[k], hy_recv.at[k], to_y(k))
+
+    def head_x(k):
+        blocks = hb.at[pl.ds(head_block(c, x, 0, 0, 0), 8)]
+        return remote(blocks, blocks, hx_send.at[k], hx_recv.at[k], to_x(k))
+
+    all_mine = hb.at[pl.ds(c * 32, 32)]
+    head_c = remote(all_mine, all_mine, hc_send, hc_recv, to_core)
+
+    ring(1, early)
     wanted = jnp.where(packed, first_row + row - OWN // 2, -1)
     pick[1] = (row_of == wanted).astype(F32).astype(BF16)
-
     place = lax.broadcasted_iota(jnp.int32, (K // 2, 1), 0)
     block = (place * 6554) >> 16
     source = ((block >> 4) & 1) * 2 + ((block >> 2) & 1) + 4 * (block & 3)
     owner = source * 4 + ((block >> 3) & 1) * 2 + c
     wanted = owner * OWN + place - block * OWN
     order[...] = (lax.broadcasted_iota(jnp.int32, (K // 2, K), 1) == wanted).astype(F32).astype(BF16)
-
-    def head_y(k):
-        blocks = hb.at[pl.ds(head_block(c, x, yl, yh, 0), 2)]
-        return remote(blocks, blocks, hy_send.at[k], hy_recv.at[k], to_y(k))
-
-    def head_x(k):
-        blocks = hb.at[pl.ds(head_block(c, x, 0, 0, 0), 8)]
-        return remote(blocks, blocks, hx_send.at[k], hx_recv.at[k], to_x(k))
-
-    all_mine = hb.at[pl.ds(c * 32, 32)]
-    head_c = remote(all_mine, all_mine, hc_send, hc_recv, to_core)
-
-    ring(1)
+    text_y[1].start()
+    ring(1, late)
     for zh in range(2):
 
         @pl.when(z != head_z0 + 8 * zh)
@@ -289,24 +298,25 @@
         load.wait()
     for copy in text_c + text_yc:
         copy.wait_recv()
+    diagonal = lax.broadcasted_iota(jnp.int32, (ROWS, ROWS), 0) == lax.broadcasted_iota(jnp.int32, (ROWS, ROWS), 1)
+    for i in range(4):
+        column = jnp.sum(jnp.where(diagonal, tl[i].astype(F32), 0.0), axis=1, keepdims=True)
+        label_wide[pl.ds(i * ROWS, ROWS)] = jnp.broadcast_to(column, (ROWS, ROWS)).astype(jnp.int32)
     features = tf[...].reshape(4 * ROWS, K)
     whole = jnp.dot(features, pick[0], preferred_element_type=F32)
     spread[0] = jnp.where(row < OWN, whole, 0.0).astype(BF16)
     spread[1] = jnp.where(row < OWN, 0.0, whole).astype(BF16)
-    spread[2] = jnp.dot(features, pick[1], preferred_element_type=F32).astype(BF16)
-    feat_t[...] = lax.dot_general(order[...], features, NT, preferred_element_type=F32).astype(BF16)
-    diagonal = lax.broadcasted_iota(jnp.int32, (ROWS, ROWS), 0) == lax.broadcasted_iota(jnp.int32, (ROWS, ROWS), 1)
-    for i in range(4):
-        column = jnp.sum(jnp.where(diagonal, tl[i].astype(F32), 0.0), axis=1, keepdims=True)
-        label_wide[pl.ds(i * ROWS, ROWS)] = jnp.broadcast_to(column, (ROWS, ROWS)).astype(jnp.int32)
-    ring(5)
+    ring(5, early)
+    spread[2] = jnp.dot(tf[...].reshape(4 * ROWS, K), pick[1], preferred_element_type=F32).astype(BF16)
+    ring(5, late)
     for k in range(1, 4):
         head_x(k).wait_recv()
     head_c.start()
+    feat_t[...] = lax.dot_general(order[...], tf[...].reshape(4 * ROWS, K), NT, preferred_element_type=F32).astype(BF16)
     ring(6, early)
     head_c.wait_recv()
     head_all = hb[...].reshape(64 * PAD, WIDE)
-    for i in range(4):
+    def project(i):
         rows = pl.ds(i * ROWS, ROWS)
         left = jnp.dot(spread[0, rows], head_all, preferred_element_type=F32)
         right = jnp.dot(spread[1, rows], head_all[:, :REST], preferred_element_type=F32)
@@ -317,6 +327,26 @@
         inv_norm[rows] = inv
         text_exact[rows] = exact
         text_unit[rows] = exact.astype(BF16)
+
+    project(0)
+    project(1)
+
+    @pl.when(is_source)
+    def _():
+        def drain_head(k, carry):
+            head_z(k).wait_send()
+            return carry
+
+        lax.fori_loop(1, NZ, drain_head, 0)
+
+    for copy in text_y + text_c + text_yc:
+        copy.wait_send()
+    for k in range(1, 4):
+        head_y(k).wait_send()
+        head_x(k).wait_send()
+    ring(6, late)
+    project(2)
+    project(3)
 
     lane = lax.broadcasted_iota(jnp.int32, (1, ROWS), 1)
 
@@ -338,7 +368,6 @@
             else:
                 unit_grad[rows] += grad
 
-    ring(6, late)
     process(0, 4, (0, -1, 1, -2), True)
     ring(7, early)
     process(4, 4, (2, -3, 3, -4))
@@ -351,30 +380,13 @@
     process(15, 1, (8,))
 
     def drain():
-        @pl.when(is_source)
-        def _():
-            def drain_head(k, carry):
-                head_z(k).wait_send()
-                return carry
-
-            lax.fori_loop(1, NZ, drain_head, 0)
-
-        for copy in text_y + text_c + text_yc + [head_c]:
-            copy.wait_send()
-        for k in range(1, 4):
-            head_y(k).wait_send()
-            head_x(k).wait_send()
-
-        def drain_ring(s, carry):
-            for k in range(CHUNKS):
-                up(s, k).wait_send()
-                dn(s, k).wait_send()
-            return carry
-
-        lax.fori_loop(1, 8, drain_ring, 0)
+        for k in range(CHUNKS):
+            up(7, k).wait_send()
+            dn(7, k).wait_send()
         for k in range(CHUNKS // 2):
             up(8, k).wait_send()
             dn(8, k + CHUNKS // 2).wait_send()
+        head_c.wait_send()
 
     def to_other(i):
         rows, there = pl.ds(i * ROWS, ROWS), pl.ds((i ^ 1) * ROWS, ROWS)
@@ -387,20 +399,27 @@
         grad_low[rows] = ((grad - exact * along) * (logit_scale * inv_norm[rows])).astype(BF16)
         to_other(i).start()
 
-    def a_x(k):
-        return remote(a_out.at[(x + k) % 4], a_in.at[k - 1], ga_send.at[0, k], ga_recv.at[0], to_x(k))
-
-    def b_y(k):
-        return remote(b_out.at[(y + k) % 4], b_in.at[k - 1], gb_send.at[0, k], gb_recv.at[0], to_y(k))
-
-    def a_y(k):
-        return remote(a2_out.at[(y + k) % 4], a2_in.at[k - 1], ga_send.at[1, k], ga_recv.at[1], to_y(k))
-
-    def b_x(k):
-        return remote(b2_out.at[(x + k) % 4], b2_in.at[k - 1], gb_send.at[1, k], gb_recv.at[1], to_x(k))
-
-    def all_in(ref, sem):
-        remote(ref, ref, ga_send.at[0, 0], sem, to_x(1)).wait_recv()
+    def x_copy(k):
+        src, dst = (x_far_out, x_far_in) if k == 2 else (x_out.at[k // 2], x_in.at[k // 2])
+        return remote(src, dst, ga_send.at[0, k], ga_recv.at[0, k], to_x(k))
+
+    def y_copy(k):
+        src, dst = (y_far_out, y_far_in) if k == 2 else (y_out.at[k // 2], y_in.at[k // 2])
+        return remote(src, dst, gb_send.at[0, k], gb_recv.at[0, k], to_y(k))
+
+    def x_last(k):
+        src, dst = (x2_far_out, x2_far_in) if k == 2 else (x2_out.at[k // 2], x2_in.at[k // 2])
+        return remote(src, dst, gb_send.at[1, k], gb_recv.at[1, k], to_x(k))
+
+    def y_last(k):
+        src, dst = (y2_far_out, y2_far_in) if k == 2 else (y2_out.at[k // 2], y2_in.at[k // 2])
+        return remote(src, dst, ga_send.at[1, k], ga_recv.at[1, k], to_y(k))
+
+    def low(parts, rows):
+        filler = rows - sum(p.shape[0] for p in parts)
+        if filler:
+            parts = parts + [jnp.zeros((filler, HALF), F32)]
+        return jnp.concatenate(parts, axis=0).astype(BF16)
 
     for h in range(2):
         partial[h] = jnp.dot(feat_t[pl.ds(h * 160, 160)], grad_low[...], preferred_element_type=F32)
@@ -408,55 +427,61 @@
         to_other(i).wait_recv()
     for h in range(2):
         mine = partial[h] + jnp.dot(feat_t[pl.ds(h * 160, 160)], grad_in[...], preferred_element_type=F32)
-        groups = [mine[k * 40 : (k + 1) * 40] for k in range(4)]
-        first = jnp.concatenate([g[:FIRST] for g in groups], axis=0)
-        for side in range(2):
-            part = first[:, side * HALF : (side + 1) * HALF]
-            a_own[2 * h + side] = part
-            a_out[2 * h + side] = part.astype(BF16)
-        for k in (2, 1, 3):
-
-            @pl.when((x + k) % 4 // 2 == h)
-            def _():
-                a_x(k).start()
-
         for k in range(4):
-            b_own[k, h] = groups[k][FIRST:]
-            b_out[k, h] = groups[k][FIRST:].astype(BF16)
-
-    for k in (2, 1, 3):
-        b_y(k).start()
+            for side in range(2):
+                piece[2 * h + side, k] = mine[k * 40 : (k + 1) * 40, side * HALF : (side + 1) * HALF]
+
+    def mine_of(dx, dy):
+        return piece.at[(x + dx) % 4, (y + dy) % 4]
+
+    top, end = pl.ds(0, FIRST), pl.ds(FIRST, SECOND)
+    for k in (1, 3):
+        x_out[k // 2] = low([mine_of(k, 0)[top], mine_of(k, 1)[top], mine_of(k, 3)[top], mine_of(k, 2)[...]], 112)
+        x_copy(k).start()
+    x_far_out[...] = low([mine_of(2, 2)[top]], 32)
+    x_copy(2).start()
+    for k in (1, 3):
+        y_out[k // 2] = low([mine_of(0, k)[end], mine_of(1, k)[end], mine_of(3, k)[end], mine_of(2, k)[...]], 96)
+        y_copy(k).start()
+    y_far_out[...] = low([mine_of(2, 2)[end]], 16)
+    y_copy(2).start()
     drain()
-    all_in(b_in, gb_recv.at[0])
-    total = b_own[y]
-    for k in range(3):
-        total += b_in[k].astype(F32)
-    for h in range(2):
-        for side in range(2):
-            part = total[h, :, side * HALF : (side + 1) * HALF]
-            b2_own[2 * h + side] = part
-            b2_out[2 * h + side] = part.astype(BF16)
-    for k in (2, 1, 3):
-        b_x(k).start()
-    all_in(a_in, ga_recv.at[0])
-    total = a_own[x]
-    for k in range(3):
-        total += a_in[k].astype(F32)
-    for k in range(4):
-        part = total[k * FIRST : (k + 1) * FIRST]
-        a2_own[k] = part
-        a2_out[k] = jnp.concatenate([part, jnp.zeros((32 - FIRST, HALF), F32)], axis=0).astype(BF16)
-    for k in (2, 1, 3):
-        a_y(k).start()
-    all_in(b2_in, gb_recv.at[1])
-    second = b2_own[x]
-    for k in range(3):
-        second += b2_in[k].astype(F32)
-    all_in(a2_in, ga_recv.at[1])
-    first = a2_own[y]
-    for k in range(3):
-        first += a2_in[k, :FIRST].astype(F32)
+
+    for k in (1, 3, 2):
+        y_copy(k).wait_recv()
+    came = y_in[0].astype(F32) + y_in[1].astype(F32)
+    x2_far_out[...] = low(
+        [mine_of(2, 0)[top] + came[48 : 48 + FIRST], mine_of(2, 0)[end] + came[48 + FIRST : 88] + y_far_in[...].astype(F32)], 48
+    )
+    x_last(2).start()
+    x2_out[0] = (mine_of(1, 0)[end] + came[16:32]).astype(BF16)
+    x_last(1).start()
+    x2_out[1] = (mine_of(3, 0)[end] + came[32:48]).astype(BF16)
+    x_last(3).start()
+    second = mine_of(0, 0)[end] + came[:16]
+
+    for k in (1, 3, 2):
+        x_copy(k).wait_recv()
+    came = x_in[0].astype(F32) + x_in[1].astype(F32)
+    y2_far_out[...] = low(
+        [mine_of(0, 2)[top] + came[72 : 72 + FIRST] + x_far_in[pl.ds(0, FIRST)].astype(F32), mine_of(0, 2)[end] + came[72 + FIRST :]],
+        48,
+    )
+    y_last(2).start()
+    y2_out[0] = low([mine_of(0, 1)[top] + came[FIRST : 2 * FIRST]], 32)
+    y_last(1).start()
+    y2_out[1] = low([mine_of(0, 3)[top] + came[2 * FIRST : 3 * FIRST]], 32)
+    y_last(3).start()
+    first = mine_of(0, 0)[top] + came[:FIRST]
+
+    for k in (1, 3, 2):
+        x_last(k).wait_recv()
+    second += x2_in[0].astype(F32) + x2_in[1].astype(F32)
+    for k in (1, 3, 2):
+        y_last(k).wait_recv()
+    first += y2_in[0, :FIRST].astype(F32) + y2_in[1, :FIRST].astype(F32)
     total = jnp.concatenate([first, second], axis=0)
+    total += x2_far_in[:40].astype(F32) + y2_far_in[:40].astype(F32)
     for j in range(4):
         part = total[j * OWN : (j + 1) * OWN]
         thirds = [part[:, i * 128 : (i + 1) * 128] for i in range(3)] + [jnp.zeros((2, 128), F32)]
@@ -501,10 +526,10 @@
     head_grad_ref[...] = jnp.concatenate(pieces, axis=1) * (1.0 / 8.0)
 
     for k in range(1, 4):
-        a_x(k).wait_send()
-        b_y(k).wait_send()
-        a_y(k).wait_send()
-        b_x(k).wait_send()
+        x_copy(k).wait_send()
+        y_copy(k).wait_send()
+        x_last(k).wait_send()
+        y_last(k).wait_send()
     for i in range(4):
         to_other(i).wait_send()
     for j in range(4):
@@ -550,18 +575,23 @@
             pltpu.VMEM((texts, D), BF16),
             pltpu.VMEM((texts, D), BF16),
             pltpu.VMEM((2, 160, D), F32),
-            pltpu.VMEM((4, 4 * FIRST, HALF), F32),
-            pltpu.VMEM((4, 4 * FIRST, HALF), BF16),
-            pltpu.VMEM((3, 4 * FIRST, HALF), BF16),
-            pltpu.VMEM((4, 2, SECOND, D), F32),
-            pltpu.VMEM((4, 2, SECOND, D), BF16),
-            pltpu.VMEM((3, 2, SECOND, D), BF16),
-            pltpu.VMEM((4, FIRST, HALF), F32),
-            pltpu.VMEM((4, 32, HALF), BF16),
-            pltpu.VMEM((3, 32, HALF), BF16),
-            pltpu.VMEM((4, SECOND, HALF), F32),
-            pltpu.VMEM((4, SECOND, HALF), BF16),
-            pltpu.VMEM((3, SECOND, HALF), BF16),
+            pltpu.VMEM((4, 4, 40, HALF), F32),
+            pltpu.VMEM((2, 112, HALF), BF16),
+            pltpu.VMEM((2, 112, HALF), BF16),
+            pltpu.VMEM((32, HALF), BF16),
+            pltpu.VMEM((32, HALF), BF16),
+            pltpu.VMEM((2, 96, HALF), BF16),
+            pltpu.VMEM((2, 96, HALF), BF16),
+            pltpu.VMEM((SECOND, HALF), BF16),
+            pltpu.VMEM((SECOND, HALF), BF16),
+            pltpu.VMEM((2, SECOND, HALF), BF16),
+            pltpu.VMEM((2, SECOND, HALF), BF16),
+            pltpu.VMEM((48, HALF), BF16),
+            pltpu.VMEM((48, HALF), BF16),
+            pltpu.VMEM((2, 32, HALF), BF16),
+            pltpu.VMEM((2, 32, HALF), BF16),
+            pltpu.VMEM((48, HALF), BF16),
+            pltpu.VMEM((48, HALF), BF16),
             pltpu.VMEM((4, 32, 128), BF16),
             pltpu.VMEM((NZ, 32, 128), BF16),
             pltpu.VMEM((2, 32, 128), F32),
@@ -583,9 +613,9 @@
             dma((4,)),
             dma((4,)),
             dma((2, 4)),
-            dma((2,)),
             dma((2, 4)),
-            dma((2,)),
+            dma((2, 4)),
+            dma((2, 4)),
             dma((4,)),
             dma,
             dma((8,)),

time: 80 us -> 79.1 us (0.989)
  Pallas kernels: 77.4 us -> 76.5 us
    pallas_call x1, Pallas kernels: 77.4 us -> 76.5 us  [per_device(): pl.pallas_call(kernel, out_shape=out, in_specs=[hbm] * 5, out_specs=vmem,...]
where the time goes in v4:
time: 79.1 us; the launch traced here: 78.6 us
  Pallas kernels  76.5 us (97%)
  other arithmetic  1.45 us (2%)
    pallas_call x1, Pallas kernels, per_device(): pl.pallas_call(kernel, out_shape=out, in_specs=[hbm] * 5, out_specs=vmem,...  76.5 us

profile of v4, /device:TPU:6, one launch (start us, length us, event | category | flops | bytes accessed | tf_op | source)
XLA Modules:
  0.0 78.6 jit_solution(10160520890431338879)
XLA Ops:
  0.6 0.0 copy-start
  0.6 0.0 copy-start.1
  0.7 76.5 %contrastive_step.1 = f32[10,768]{1,0:T(8,128)} custom-call(bf16[128,768]{1,0:T(8,128)(2,1)} %bitcast.3, bf16[128,768]{1,0:T(8,128)(2,1)} %bitcast.4, bf16[128,640]{1,0:T(8,128)(2,1)} %bitcast.5, f32[10,768]{1,0:T(8,128)} %head_hbm.1, s32[1,128]{1,0:T(1,128)} %label_hbm.1), custom_call_target="tpu_custom_call" | custom-call | flops 8000000000 | bytes 2000000 | tf_op jit(solution)/shard_map/contrastive_step/pallas_call | solution.py:553
  77.2 0.0 copy-done
  77.2 0.0 copy-done.1
  77.2 1.4 %multiply_subtract_fusion = (f32[10,768]{1,0:T(8,128)}, f32[10,768]{1,0:T(8,128)}) fusion(f32[10,768]{1,0:T(8,128)S(1)} %copy-done, f32[10,768]{1,0:T(8,128)} %contrastive_step.1, f32[10,768]{1,0:T(8,128)S(1)} %copy-done.1), kind=kLoop, calls=%fused_computation | loop fusion | flops 61440 | bytes 153600 | tf_op jit(solution)/shard_map/sub | solution.py:631
Async XLA Ops:
  0.6 76.5 %copy-start = (f32[10,768]{1,0:T(8,128)S(1)}, f32[10,768]{1,0:T(8,128)}, u32[]{:S(2)}) copy-start(f32[10,768]{1,0:T(8,128)} %head_hbm.1) | copy-start | bytes 92164
  0.6 76.5 %copy-start.1 = (f32[10,768]{1,0:T(8,128)S(1)}, f32[10,768]{1,0:T(8,128)}, u32[]{:S(2)}) copy-start(f32[10,768]{1,0:T(8,128)} %param.10) | copy-start | bytes 92164

commit v5 on v4

--- a/solution.py
+++ b/solution.py
@@ -67,8 +67,6 @@
     x_far_in,
     y_out,
     y_in,
-    y_far_out,
-    y_far_in,
     x2_out,
     x2_in,
     x2_far_out,
@@ -389,23 +387,23 @@
         head_c.wait_send()
 
     def to_other(i):
-        rows, there = pl.ds(i * ROWS, ROWS), pl.ds((i ^ 1) * ROWS, ROWS)
-        return remote(grad_low.at[rows], grad_in.at[there], gc_send.at[i], gc_recv.at[i], to_core)
+        rows = pl.ds(2 * i, 2)
+        return remote(grad_low.at[rows], grad_in.at[rows], gc_send.at[i], gc_recv.at[i], to_core)
 
     for i in range(4):
         rows = pl.ds(i * ROWS, ROWS)
         exact, grad = text_exact[rows], unit_grad[rows]
         along = jnp.sum(exact * grad, axis=1, keepdims=True)
-        grad_low[rows] = ((grad - exact * along) * (logit_scale * inv_norm[rows])).astype(BF16)
-        to_other(i).start()
+        grad_low[i] = ((grad - exact * along) * (logit_scale * inv_norm[rows])).astype(BF16)
+        if i % 2 == 1:
+            to_other(i // 2).start()
 
     def x_copy(k):
         src, dst = (x_far_out, x_far_in) if k == 2 else (x_out.at[k // 2], x_in.at[k // 2])
         return remote(src, dst, ga_send.at[0, k], ga_recv.at[0, k], to_x(k))
 
     def y_copy(k):
-        src, dst = (y_far_out, y_far_in) if k == 2 else (y_out.at[k // 2], y_in.at[k // 2])
-        return remote(src, dst, gb_send.at[0, k], gb_recv.at[0, k], to_y(k))
+        return remote(y_out.at[k // 2], y_in.at[k // 2], gb_send.at[0, k], gb_recv.at[0, k], to_y(k))
 
     def x_last(k):
         src, dst = (x2_far_out, x2_far_in) if k == 2 else (x2_out.at[k // 2], x2_in.at[k // 2])
@@ -422,11 +420,12 @@
         return jnp.concatenate(parts, axis=0).astype(BF16)
 
     for h in range(2):
-        partial[h] = jnp.dot(feat_t[pl.ds(h * 160, 160)], grad_low[...], preferred_element_type=F32)
-    for i in range(4):
+        partial[h] = jnp.dot(feat_t[pl.ds(h * 160, 160)], grad_low[...].reshape(4 * ROWS, D), preferred_element_type=F32)
+    for i in range(2):
         to_other(i).wait_recv()
+    others_grad = jnp.concatenate([grad_in[i ^ 1] for i in range(4)], axis=0)
     for h in range(2):
-        mine = partial[h] + jnp.dot(feat_t[pl.ds(h * 160, 160)], grad_in[...], preferred_element_type=F32)
+        mine = partial[h] + jnp.dot(feat_t[pl.ds(h * 160, 160)], others_grad, preferred_element_type=F32)
         for k in range(4):
             for side in range(2):
                 piece[2 * h + side, k] = mine[k * 40 : (k + 1) * 40, side * HALF : (side + 1) * HALF]
@@ -438,20 +437,18 @@
     for k in (1, 3):
         x_out[k // 2] = low([mine_of(k, 0)[top], mine_of(k, 1)[top], mine_of(k, 3)[top], mine_of(k, 2)[...]], 112)
         x_copy(k).start()
-    x_far_out[...] = low([mine_of(2, 2)[top]], 32)
+    x_far_out[...] = low([mine_of(2, 2)[...]], 48)
     x_copy(2).start()
     for k in (1, 3):
         y_out[k // 2] = low([mine_of(0, k)[end], mine_of(1, k)[end], mine_of(3, k)[end], mine_of(2, k)[...]], 96)
         y_copy(k).start()
-    y_far_out[...] = low([mine_of(2, 2)[end]], 16)
-    y_copy(2).start()
     drain()
 
-    for k in (1, 3, 2):
+    for k in (1, 3):
         y_copy(k).wait_recv()
     came = y_in[0].astype(F32) + y_in[1].astype(F32)
     x2_far_out[...] = low(
-        [mine_of(2, 0)[top] + came[48 : 48 + FIRST], mine_of(2, 0)[end] + came[48 + FIRST : 88] + y_far_in[...].astype(F32)], 48
+        [mine_of(2, 0)[top] + came[48 : 48 + FIRST], mine_of(2, 0)[end] + came[48 + FIRST : 88]], 48
     )
     x_last(2).start()
     x2_out[0] = (mine_of(1, 0)[end] + came[16:32]).astype(BF16)
@@ -463,10 +460,8 @@
     for k in (1, 3, 2):
         x_copy(k).wait_recv()
     came = x_in[0].astype(F32) + x_in[1].astype(F32)
-    y2_far_out[...] = low(
-        [mine_of(0, 2)[top] + came[72 : 72 + FIRST] + x_far_in[pl.ds(0, FIRST)].astype(F32), mine_of(0, 2)[end] + came[72 + FIRST :]],
-        48,
-    )
+    far_in = x_far_in[...].astype(F32)
+    y2_far_out[...] = low([mine_of(0, 2)[...] + came[72:] + far_in[:40]], 48)
     y_last(2).start()
     y2_out[0] = low([mine_of(0, 1)[top] + came[FIRST : 2 * FIRST]], 32)
     y_last(1).start()
@@ -527,10 +522,11 @@
 
     for k in range(1, 4):
         x_copy(k).wait_send()
-        y_copy(k).wait_send()
+        if k != 2:
+            y_copy(k).wait_send()
         x_last(k).wait_send()
         y_last(k).wait_send()
-    for i in range(4):
+    for i in range(2):
         to_other(i).wait_send()
     for j in range(4):
 
@@ -572,18 +568,16 @@
             pltpu.VMEM((texts, 1), F32),
             pltpu.VMEM((texts, ROWS), jnp.int32),
             pltpu.VMEM((texts, D), F32),
-            pltpu.VMEM((texts, D), BF16),
-            pltpu.VMEM((texts, D), BF16),
+            pltpu.VMEM((4, ROWS, D), BF16),
+            pltpu.VMEM((4, ROWS, D), BF16),
             pltpu.VMEM((2, 160, D), F32),
             pltpu.VMEM((4, 4, 40, HALF), F32),
             pltpu.VMEM((2, 112, HALF), BF16),
             pltpu.VMEM((2, 112, HALF), BF16),
-            pltpu.VMEM((32, HALF), BF16),
-            pltpu.VMEM((32, HALF), BF16),
+            pltpu.VMEM((48, HALF), BF16),
+            pltpu.VMEM((48, HALF), BF16),
             pltpu.VMEM((2, 96, HALF), BF16),
             pltpu.VMEM((2, 96, HALF), BF16),
-            pltpu.VMEM((SECOND, HALF), BF16),
-            pltpu.VMEM((SECOND, HALF), BF16),
             pltpu.VMEM((2, SECOND, HALF), BF16),
             pltpu.VMEM((2, SECOND, HALF), BF16),
             pltpu.VMEM((48, HALF), BF16),

time: 79.1 us -> 79.1 us (level)
  no operation moved by 1% of the time
where the time goes in v5:
time: 79.1 us; the launch traced here: 78.5 us
  Pallas kernels  76.4 us (97%)
  other arithmetic  1.45 us (2%)
    pallas_call x1, Pallas kernels, per_device(): pl.pallas_call(kernel, out_shape=out, in_specs=[hbm] * 5, out_specs=vmem,...  76.4 us

profile of v5, /device:TPU:6, one launch (start us, length us, event | category | flops | bytes accessed | tf_op | source)
XLA Modules:
  0.0 78.5 jit_solution(1384961082385383120)
XLA Ops:
  0.6 0.0 copy-start
  0.6 0.0 copy-start.1
  0.7 76.4 %contrastive_step.1 = f32[10,768]{1,0:T(8,128)} custom-call(bf16[128,768]{1,0:T(8,128)(2,1)} %bitcast.3, bf16[128,768]{1,0:T(8,128)(2,1)} %bitcast.4, bf16[128,640]{1,0:T(8,128)(2,1)} %bitcast.5, f32[10,768]{1,0:T(8,128)} %head_hbm.1, s32[1,128]{1,0:T(1,128)} %label_hbm.1), custom_call_target="tpu_custom_call" | custom-call | flops 8000000000 | bytes 2000000 | tf_op jit(solution)/shard_map/contrastive_step/pallas_call | solution.py:549
  77.0 0.0 copy-done
  77.0 0.0 copy-done.1
  77.0 1.4 %multiply_subtract_fusion = (f32[10,768]{1,0:T(8,128)}, f32[10,768]{1,0:T(8,128)}) fusion(f32[10,768]{1,0:T(8,128)S(1)} %copy-done, f32[10,768]{1,0:T(8,128)} %contrastive_step.1, f32[10,768]{1,0:T(8,128)S(1)} %copy-done.1), kind=kLoop, calls=%fused_computation | loop fusion | flops 61440 | bytes 153600 | tf_op jit(solution)/shard_map/sub | solution.py:625
Async XLA Ops:
  0.6 76.4 %copy-start = (f32[10,768]{1,0:T(8,128)S(1)}, f32[10,768]{1,0:T(8,128)}, u32[]{:S(2)}) copy-start(f32[10,768]{1,0:T(8,128)} %head_hbm.1) | copy-start | bytes 92164
  0.6 76.4 %copy-start.1 = (f32[10,768]{1,0:T(8,128)S(1)}, f32[10,768]{1,0:T(8,128)}, u32[]{:S(2)}) copy-start(f32[10,768]{1,0:T(8,128)} %param.10) | copy-start | bytes 92164

commit v6 on v4

--- a/solution.py
+++ b/solution.py
@@ -372,8 +372,7 @@
     ring(7, early)
     process(4, 4, (2, -3, 3, -4))
     ring(7, late)
-    process(8, 4, (4, -5, 5, -6))
-    process(12, 3, (6, -7, 7))
+    process(8, 7, (4, -5, 5, -6, 6, -7, 7))
     for k in range(CHUNKS // 2):
         up(8, k).wait_recv()
         dn(8, k + CHUNKS // 2).wait_recv()

time: 79.1 us -> 79.1 us (level)
  no operation moved by 1% of the time
where the time goes in v6:
time: 79.1 us; the launch traced here: 78.7 us
  Pallas kernels  76.5 us (97%)
  other arithmetic  1.45 us (2%)
    pallas_call x1, Pallas kernels, per_device(): pl.pallas_call(kernel, out_shape=out, in_specs=[hbm] * 5, out_specs=vmem,...  76.5 us

profile of v6, /device:TPU:6, one launch (start us, length us, event | category | flops | bytes accessed | tf_op | source)
XLA Modules:
  0.0 78.7 jit_solution(3612254675237912010)
XLA Ops:
  0.6 0.0 copy-start
  0.6 0.0 copy-start.1
  0.7 76.5 %contrastive_step.1 = f32[10,768]{1,0:T(8,128)} custom-call(bf16[128,768]{1,0:T(8,128)(2,1)} %bitcast.3, bf16[128,768]{1,0:T(8,128)(2,1)} %bitcast.4, bf16[128,640]{1,0:T(8,128)(2,1)} %bitcast.5, f32[10,768]{1,0:T(8,128)} %head_hbm.1, s32[1,128]{1,0:T(1,128)} %label_hbm.1), custom_call_target="tpu_custom_call" | custom-call | flops 8000000000 | bytes 2000000 | tf_op jit(solution)/shard_map/contrastive_step/pallas_call | solution.py:552
  77.2 0.0 copy-done
  77.2 0.0 copy-done.1
  77.2 1.4 %multiply_subtract_fusion = (f32[10,768]{1,0:T(8,128)}, f32[10,768]{1,0:T(8,128)}) fusion(f32[10,768]{1,0:T(8,128)S(1)} %copy-done, f32[10,768]{1,0:T(8,128)} %contrastive_step.1, f32[10,768]{1,0:T(8,128)S(1)} %copy-done.1), kind=kLoop, calls=%fused_computation | loop fusion | flops 61440 | bytes 153600 | tf_op jit(solution)/shard_map/sub | solution.py:630
Async XLA Ops:
  0.6 76.6 %copy-start = (f32[10,768]{1,0:T(8,128)S(1)}, f32[10,768]{1,0:T(8,128)}, u32[]{:S(2)}) copy-start(f32[10,768]{1,0:T(8,128)} %head_hbm.1) | copy-start | bytes 92164
  0.6 76.6 %copy-start.1 = (f32[10,768]{1,0:T(8,128)S(1)}, f32[10,768]{1,0:T(8,128)}, u32[]{:S(2)}) copy-start(f32[10,768]{1,0:T(8,128)} %param.10) | copy-start | bytes 92164
